TPU v7x, 32 devices: a whole 2x2x4 slice. The times are simulated.
32 devices in a mesh: seq: 8 (over z, y), head: 4 (over x, core).
Axes of the slice: x: 2, y: 2, z: 4, core: 2. Of those that a mesh axis runs over, the one named last changes fastest.
Arguments:
- hidden_states: bfloat16 [8, 5, 8192], P(None, None, 'seq'), may hold values from -6 to 6
- w_query: bfloat16 [8192, 8192], P('seq', 'head'), may hold values from -0.0625 to 0.0625
- w_key: bfloat16 [8192, 1024], P('seq', 'head'), may hold values from -0.15625 to 0.15625
- w_value: bfloat16 [8192, 1024], P('seq', 'head'), may hold values from -0.0625 to 0.0625
- w_out: bfloat16 [8192, 8192], P('head', 'seq'), may hold values from -0.0625 to 0.0625
- key_cache: bfloat16 [8, 8192, 1024], P(None, 'seq', 'head'), may hold values from -104 to 104
- value_cache: bfloat16 [8, 8192, 1024], P(None, 'seq', 'head'), may hold values from -6 to 6
- context_lengths: int32 [8], replicated, may hold values from 2048 to 8192, as said below
- keep_blocks: int32 [8, 64], P(None, 'seq'), may hold values from 0 to 1, as said below
Outputs:
- verify_out: bfloat16 [8, 5, 8192], P(None, None, 'seq')
- draft_out: bfloat16 [8, 4, 8192], P(None, None, 'seq')
Inputs may be any that keep to these rules, and one draw needn't show every extreme that they name: `keep_blocks`: block 0 of every sequence is kept. `context_lengths`: one sequence has length 8192.
All inputs are finite; a program needn't handle non-finite values.
Results may differ from a plain program's by a relative error of at most 0.017.
Values may be sent and summed in bfloat16 or wider, within the bound.
A program may use at most 64 MiB of HBM per device.

v0:
```python
import jax
import jax.numpy as jnp
from jax import lax
from jax.sharding import PartitionSpec as P

HEAD_DIM = 128
BLOCK = 128


big_negative = -1e30


def rotate(values_in, positions):
    half_dim = HEAD_DIM // 2
    inverse = 500000.0 ** (-(jnp.arange(half_dim, dtype=jnp.float32) * 2.0) / HEAD_DIM)
    angles = positions[:, :, None, None].astype(jnp.float32) * inverse
    cosine = jnp.cos(angles)
    sine = jnp.sin(angles)
    first_half = values_in[..., :half_dim]
    second_half = values_in[..., half_dim:]
    return jnp.concatenate(
        [first_half * cosine - second_half * sine, second_half * cosine + first_half * sine],
        axis=-1,
    )


def partial_softmax(scores, mask_full, cache_values):
    masked = jnp.where(mask_full, scores, big_negative)
    peak_value = jnp.max(masked, axis=-1)
    weights = jnp.where(mask_full, jnp.exp(masked - peak_value[..., None]), 0.0)
    weighted = jnp.einsum(
        "bkjgt,btkd->bkjgd",
        weights.astype(jnp.bfloat16),
        cache_values,
        preferred_element_type=jnp.float32,
    )
    return (peak_value, jnp.sum(weights, axis=-1), weighted)


def finish(partials, new_scores, causal, new_values):
    peak_cache, total_sum, weighted = partials
    mask_full = causal[None, None, :, None, :]
    masked = jnp.where(mask_full, new_scores, big_negative)
    peak_value = jnp.maximum(peak_cache, jnp.max(masked, axis=-1))
    factor_old = jnp.exp(peak_cache - peak_value)
    weights = jnp.where(mask_full, jnp.exp(masked - peak_value[..., None]), 0.0)
    total_sum = total_sum * factor_old + jnp.sum(weights, axis=-1)
    weighted = weighted * factor_old[..., None] + jnp.einsum(
        "bkjgi,bikd->bkjgd",
        weights.astype(jnp.bfloat16),
        new_values,
        preferred_element_type=jnp.float32,
    )
    result = weighted / total_sum[..., None]
    batch_size, kv_local, positions_count, group_size, head_size = result.shape
    return result.transpose(0, 2, 1, 3, 4).reshape(
        batch_size * positions_count, kv_local * group_size * head_size
    )


def per_device(
    hidden_states,
    w_query,
    w_key,
    w_value,
    w_out,
    key_cache,
    value_cache,
    context_lengths,
    keep_blocks,
):
    seq_index = lax.axis_index("seq")
    batch_size, verify, width_local = hidden_states.shape
    draft_len = verify - 1
    kv_local = key_cache.shape[2] // HEAD_DIM
    heads_local = w_query.shape[1] // HEAD_DIM
    group_size = heads_local // kv_local
    ctx_local = key_cache.shape[1]
    score_scale = HEAD_DIM ** (-0.5)
    tok_rows = hidden_states.reshape(batch_size * verify, width_local)
    query_part = jnp.dot(tok_rows, w_query, preferred_element_type=jnp.float32)
    key_part = jnp.dot(tok_rows, w_key, preferred_element_type=jnp.float32)
    value_part = jnp.dot(tok_rows, w_value, preferred_element_type=jnp.float32)
    query_sum, key_sum, value_sum = lax.psum((query_part, key_part, value_part), "seq")
    positions = context_lengths[:, None] + jnp.arange(verify, dtype=jnp.int32)[None, :]
    query_rot = rotate(
        query_sum.reshape(batch_size, verify, heads_local, HEAD_DIM), positions
    ).astype(jnp.bfloat16)
    new_key = rotate(key_sum.reshape(batch_size, verify, kv_local, HEAD_DIM), positions).astype(
        jnp.bfloat16
    )
    new_values = value_sum.reshape(batch_size, verify, kv_local, HEAD_DIM).astype(jnp.bfloat16)
    grouped = query_rot.reshape(batch_size, verify, kv_local, group_size, HEAD_DIM)
    cache_keys = key_cache.reshape(batch_size, ctx_local, kv_local, HEAD_DIM)
    cache_values = value_cache.reshape(batch_size, ctx_local, kv_local, HEAD_DIM)
    scores = (
        jnp.einsum("bjkgd,btkd->bkjgt", grouped, cache_keys, preferred_element_type=jnp.float32)
        * score_scale
    )
    key_positions = seq_index * ctx_local + jnp.arange(ctx_local, dtype=jnp.int32)
    live_mask = key_positions[None, :] < context_lengths[:, None]
    kept_mask = live_mask & (jnp.repeat(keep_blocks, BLOCK, axis=1) > 0)
    target_peak, target_total, target_weighted = partial_softmax(
        scores, live_mask[:, None, None, None, :], cache_values
    )
    draft_peak, draft_total, draft_weighted = partial_softmax(
        scores[:, :, :draft_len], kept_mask[:, None, None, None, :], cache_values
    )
    peak_target, peak_draft = lax.pmax((target_peak, draft_peak), "seq")
    factor_target = jnp.exp(target_peak - peak_target)
    factor_draft = jnp.exp(draft_peak - peak_draft)
    sum_parts = lax.psum(
        (
            target_total * factor_target,
            target_weighted * factor_target[..., None],
            draft_total * factor_draft,
            draft_weighted * factor_draft[..., None],
        ),
        "seq",
    )
    merged = (peak_target, sum_parts[0], sum_parts[1], peak_draft, sum_parts[2], sum_parts[3])
    causal = jnp.arange(verify)[None, :] <= jnp.arange(verify)[:, None]
    new_scores = (
        jnp.einsum("bjkgd,bikd->bkjgi", grouped, new_key, preferred_element_type=jnp.float32)
        * score_scale
    )
    target_heads = finish(merged[0:3], new_scores, causal, new_values)
    draft_heads = finish(merged[3:6], new_scores[:, :, :draft_len], causal[:draft_len], new_values)
    attended = jnp.concatenate([target_heads, draft_heads], axis=0).astype(jnp.bfloat16)
    projected = jnp.dot(attended, w_out, preferred_element_type=jnp.float32)
    summed = lax.psum(projected.astype(jnp.bfloat16), "head")
    verify_out = summed[: batch_size * verify].reshape(batch_size, verify, summed.shape[1])
    draft_out = summed[batch_size * verify :].reshape(batch_size, draft_len, summed.shape[1])
    return (verify_out, draft_out)


def solution(mesh):
    placed = (
        P(None, None, "seq"),
        P("seq", "head"),
        P("seq", "head"),
        P("seq", "head"),
        P("head", "seq"),
        P(None, "seq", "head"),
        P(None, "seq", "head"),
        P(),
        P(None, "seq"),
    )
    return jax.shard_map(
        per_device,
        mesh=mesh,
        in_specs=placed,
        out_specs=(P(None, None, "seq"), P(None, None, "seq")),
        check_vma=False,
    )
```

profile of v0, /device:TPU:0, one launch (start us, length us, event | category | flops | bytes accessed | tf_op | source)
XLA Modules:
  0.0 303.9 jit_solution(1546525129376017676)
XLA Ops:
  7.2 1.0 copy.78
  8.3 3.1 %convolution_bitcast_fusion = f32[5,8,16,128]{3,1,2,0:T(8,128)S(1)} fusion(bf16[40,1024]{1,0:T(8,128)(2,1)S(1)} %reshape.157, bf16[1024,2048]{1,0:T(8,128)(2,1)} %param.10), kind=kOutput, calls=%fused_computation.22 | convolution fusion | flops 167772160 | bytes 4603904 | tf_op jit(solution)/shard_map/dot_general | solution.py:81
  14.7 7.0 %reshape.159 = bf16[8,1024,2,128]{3,2,1,0:T(2,128)(2,1)} reshape(bf16[8,1024,256]{2,1,0:T(8,128)(2,1)} %param.14) | data formatting | bytes 8388608 | tf_op jit(solution)/shard_map/reshape | solution.py:94
  21.7 6.9 %reshape.160 = bf16[8,1024,2,128]{3,2,1,0:T(2,128)(2,1)} reshape(bf16[8,1024,256]{2,1,0:T(8,128)(2,1)} %param.15) | data formatting | bytes 8388608 | tf_op jit(solution)/shard_map/reshape | solution.py:95
  28.9 57.1 %all-reduce.8.cloned.1.call-done = f32[8,5,16,128]{3,2,1,0:T(8,128)} async-done(((f32[8,5,16,128]{3,2,1,0:T(8,128)}), f32[8,5,16,128]{3,2,1,0:T(8,128)}) %all-reduce.8.cloned.1.call-update) | async-done | bytes 327696 | tf_op jit(solution)/shard_map/psum | solution.py:84
  86.0 1.2 fusion.41
  87.3 3.8 %select_reduce_fusion = (f32[8,2,5,8]{3,2,1,0:T(8,128)S(1)}, f32[8,2,5,8,1024]{4,3,2,1,0:T(8,128)S(1)}) fusion(pred[8,1024]{1,0:T(8,128)(4,1)S(1)} %get-tuple-element.38, bf16[8,1024,2,128,1]{3,2,1,0,4:T(2,128)(2,1)} %bitcast.40, bf16[8,5,2,8,64]{4,3,2,1,0:T(8,128)(2,1)S(1)} %get-tuple-element.31, bf16[8,5,2,8,64]{4,3,2,1,0:T(8,128)(2,1)S(1)} %get-tuple-element.30), kind=kOutput, calls=%fused_computation.7 | convolution fusion | flops 170065280 | bytes 6990336 | tf_op jit(solution)/shard_map/bjkgd,btkd->bkjgt/dot_general | solution.py:97
  92.0 1.3 fusion.12
  93.3 1.4 fusion.6
  94.6 36.8 %all-reduce.2 = (f32[8,2,4,8]{3,2,1,0:T(4,128)}, f32[8,2,5,8]{3,2,1,0:T(8,128)}) all-reduce(f32[8,2,4,8]{3,2,1,0:T(4,128)} %copy-done.3, f32[8,2,5,8]{3,2,1,0:T(8,128)S(1)} %get-tuple-element.42), channel_id=1, replica_groups=mesh['seq'=8,'head'=4] {'seq'}, use_global_device_ids=true, to_apply=%region_11.12 | all-reduce | flops 1152 | bytes 9216 | tf_op jit(solution)/shard_map/pmax | solution.py:109
  131.5 1.5 fusion.63
  133.0 1.4 fusion.64
  134.4 36.7 %all-reduce.13 = (f32[8,5,2,128]{3,1,2,0:T(8,128)}, f32[8,2,4,8]{3,2,1,0:T(4,128)}, bf16[40,256]{1,0:T(8,128)(2,1)}, f32[8,2,5,8]{3,2,1,0:T(8,128)}) all-reduce(f32[8,5,2,128]{3,1,2,0:T(8,128)} %copy.83, f32[8,2,4,8]{3,2,1,0:T(4,128)} %bitcast.47, f32[40,256]{1,0:T(8,128)} %fusion.66, ...), channel_id=1, replica_groups=mesh['seq'=8,'head'=4] {'seq'}, use_global_device_ids=true, to_apply=%region_4.5 | all-reduce | flops 21632 | bytes 152576 | tf_op jit(solution)/shard_map/psum | solution.py:84
  171.2 1.0 subtract_convert_fusion.1
  173.7 1.3 convert_element_type.38
  178.0 2.0 fusion.51
  180.0 4.0 %fusion.27 = f32[8,2,4,8,128]{4,3,2,1,0:T(8,128)} fusion(bf16[8,1024,2,128,1]{3,2,1,0,4:T(2,128)(2,1)} %bitcast.41, f32[8,2,5,8,1024]{4,3,2,1,0:T(8,128)S(1)} %get-tuple-element.43, f32[8,2,4,8]{3,2,1,0:T(4,128)} %copy-done.3, pred[8,1024]{1,0:T(8,128)(4,1)S(1)} %get-tuple-element.39, f32[8,2,4,8]{3,2,1,0:T(4,128)} %bitcast.48), kind=kOutput, calls=%fused_computation.27 | convolution fusion | flops 136380416 | bytes 6565888 | tf_op jit(solution)/shard_map/bkjgt,btkd->bkjgd/dot_general | solution.py:31
  184.1 1.9 fusion.20
  186.9 0.9 fusion.44
  188.7 69.1 %all-reduce.12.cloned.1.call-done = (f32[8,2,4,8,128]{4,3,2,1,0:T(8,128)}, f32[8,2,5,8,128]{4,3,2,1,0:T(8,128)}) async-done(((f32[8,2,4,8,128]{4,3,2,1,0:T(8,128)}, f32[8,2,5,8,128]{4,3,2,1,0:T(8,128)}), (f32[8,2,4,8,128]{4,3,2,1,0:T(8,128)}, f32[8,2,5,8,128]{4,3,2,1,0:T(8,128)})) %all-reduce.12.cloned.1.call-update) | async-done | bytes 589840 | tf_op jit(solution)/shard_map/psum | solution.py:112
  257.8 1.3 fusion.32
  259.2 1.3 fusion.31
  260.6 3.7 %convolution_convert_fusion = bf16[72,1024]{1,0:T(8,128)(2,1)} fusion(bf16[2048,1024]{1,0:T(8,128)(2,1)} %param.13, bf16[32,2048]{1,0:T(8,128)(2,1)S(1)} %reshape.163, bf16[40,2048]{1,0:T(8,128)(2,1)S(1)} %reshape.162), kind=kOutput, calls=%fused_computation.28 | convolution fusion | flops 302653440 | bytes 4636672 | tf_op jit(solution)/shard_map/dot_general | solution.py:130
  264.4 29.9 %all-reduce.10.cloned.1.call-done = bf16[72,1024]{1,0:T(8,128)(2,1)} async-done(((bf16[72,1024]{1,0:T(8,128)(2,1)}), bf16[72,1024]{1,0:T(8,128)(2,1)}) %all-reduce.10.cloned.1.call-update) | async-done | bytes 147472 | tf_op jit(solution)/shard_map/psum | solution.py:131
  (68 shorter events, 14.1 us)
Async XLA Ops:
  7.2 5.8 %copy-start = (bf16[1024,256]{1,0:T(8,128)(2,1)S(1)}, bf16[1024,256]{1,0:T(8,128)(2,1)}, u32[]{:S(2)}) copy-start(bf16[1024,256]{1,0:T(8,128)(2,1)} %param.12) | copy-start | bytes 1572868
  7.2 78.9 %all-reduce.8.cloned.1.call-start = ((), (), s32[]{:S(2)}) async-start(), calls=%async_computation | async-start | bytes 655360 | tf_op jit(solution)/shard_map/psum | solution.py:84
  8.3 4.6 %copy-start.12 = (s32[8,8]{1,0:T(8,128)S(1)}, s32[8,8]{1,0:T(8,128)}, u32[]{:S(2)}) copy-start(s32[8,8]{1,0:T(8,128)} %param.17) | copy-start | bytes 772
  8.3 4.6 %copy-start.13 = (s32[8]{0:T(128)S(1)}, s32[8]{0:T(128)}, u32[]{:S(2)}) copy-start(s32[8]{0:T(128)} %param.16) | copy-start | bytes 100
  8.3 5.5 %copy-start.4 = (bf16[1024,256]{1,0:T(8,128)(2,1)S(1)}, bf16[1024,256]{1,0:T(8,128)(2,1)}, u32[]{:S(2)}) copy-start(bf16[1024,256]{1,0:T(8,128)(2,1)} %param.11) | copy-start | bytes 1572868
  12.2 245.6 %all-reduce.12.cloned.1.call-start = ((), (), s32[]{:S(2)}) async-start(), calls=%async_computation.2 | async-start | bytes 1179648 | tf_op jit(solution)/shard_map/psum | solution.py:112
  12.3 0.7 copy-start.10
  28.9 58.4 %copy-start.6 = (f32[8,5,64]{2,1,0:T(8,128)}, f32[8,5,64]{2,1,0:T(8,128)S(1)}, u32[]{:S(2)}) copy-start(f32[8,5,64]{2,1,0:T(8,128)S(1)} %get-tuple-element.40) | copy-start | bytes 30724
  28.9 58.4 %copy-start.7 = (f32[8,5,64]{2,1,0:T(8,128)}, f32[8,5,64]{2,1,0:T(8,128)S(1)}, u32[]{:S(2)}) copy-start(f32[8,5,64]{2,1,0:T(8,128)S(1)} %get-tuple-element.41) | copy-start | bytes 30724
  91.4 0.6 copy-start.3
  175.7 8.3 %copy-start.5 = (f32[8,2,4,8]{3,0,2,1:T(8,128)}, f32[8,2,4,8]{3,0,2,1:T(8,128)S(1)}, u32[]{:S(2)}) copy-start(f32[8,2,4,8]{3,0,2,1:T(8,128)S(1)} %fusion.46) | copy-start | bytes 6148
  180.0 4.0 %copy-start.1 = (bf16[8,1024,2,128]{3,2,1,0:T(2,128)(2,1)S(1)}, bf16[8,1024,2,128]{3,2,1,0:T(2,128)(2,1)}, u32[]{:S(2)}) copy-start(bf16[8,1024,2,128]{3,2,1,0:T(2,128)(2,1)} %reshape.160) | copy-start | bytes 12582916
  180.0 4.0 %copy-start.8 = (f32[8,2,5,8]{3,2,1,0:T(8,128)S(1)}, f32[8,2,5,8]{3,2,1,0:T(8,128)}, u32[]{:S(2)}) copy-start(f32[8,2,5,8]{3,2,1,0:T(8,128)} %get-tuple-element.27) | copy-start | bytes 7684
  184.1 2.8 copy-start.11
  184.1 3.7 %copy-start.2 = (f32[8,2,5,8]{3,2,1,0:T(8,128)S(1)}, f32[8,2,5,8]{3,2,1,0:T(8,128)}, u32[]{:S(2)}) copy-start(f32[8,2,5,8]{3,2,1,0:T(8,128)} %get-tuple-element.19) | copy-start | bytes 7684
  186.0 73.2 %copy-start.9 = (bf16[8,5,2,128]{3,2,1,0:T(2,128)(2,1)S(1)}, bf16[8,5,2,128]{3,2,1,0:T(2,128)(2,1)}, u32[]{:S(2)}) copy-start(bf16[8,5,2,128]{3,2,1,0:T(2,128)(2,1)} %convert_element_type.38) | copy-start | bytes 61444
  186.0 108.2 %all-reduce.10.cloned.1.call-start = ((), (), s32[]{:S(2)}) async-start(), calls=%async_computation.1 | async-start | bytes 294912 | tf_op jit(solution)/shard_map/psum | solution.py:131
Sparse Core Ops, SparseCore 0:
  12.3 73.6 all-reduce.7
  186.1 71.6 all-reduce.11
  264.5 29.6 all-reduce.9
where the time goes:
time: 305 us; the launch traced here: 304 us
  waiting for transfers between devices  156 us (51%)
  blocking collectives  73.6 us (24%)
  local copies, waits for them, and re-layouts  23 us (8%)
  matrix products  20.9 us (7%)
  other arithmetic  16.2 us (5%)
  between operations  14 us (5%)
    psum x1, waiting for transfers between devices, per_device(): lax.psum((target_total * factor_target, target_weighted * factor_target[....  69.1 us
    psum x1, waiting for transfers between devices, per_device(): lax.psum((query_part, key_part, value_part), 'seq')  57.1 us
    pmax x1, blocking collectives, per_device(): peak_target, peak_draft = lax.pmax((target_peak, draft_peak), 'seq')  36.8 us
    psum x1, blocking collectives, per_device(): lax.psum((query_part, key_part, value_part), 'seq')  36.7 us
    psum x1, waiting for transfers between devices, per_device(): summed = lax.psum(projected.astype(jnp.bfloat16), 'head')  29.9 us
    reshape x1, local copies, waits for them, and re-layouts, per_device(): cache_keys = key_cache.reshape(batch_size, ctx_local, kv_local, HEAD_DIM)  6.98 us
    reshape x1, local copies, waits for them, and re-layouts, per_device(): value_cache.reshape(batch_size, ctx_local, kv_local, HEAD_DIM)  6.93 us
  transfers between devices with their start and end apart: 3, of which 3 were waited for; matrix products, arithmetic and copies ran while one was open for 6% of the time, Pallas kernels for 0%

commit v1 on v0

v1 whole, which is shorter than its diff:
```python
import functools
import math

import jax
import jax.numpy as jnp
import numpy as np
from jax import lax
from jax.experimental import pallas as pl
from jax.experimental.pallas import tpu as pltpu
from jax.sharding import PartitionSpec as P

HEAD_DIM = 128
BLOCK = 128
NEG = -1e30
MESH = pl.DeviceIdType.MESH
F32 = jnp.float32
BF16 = jnp.bfloat16


def round_up(value, unit):
    return -(-value // unit) * unit


def kernel(
    dims,
    hid,
    inv,
    ctx,
    keep,
    wq,
    wk,
    wv,
    wo,
    kc,
    vc,
    out,
    w_buf,
    wo_buf,
    k_buf,
    v_buf,
    hs,
    part,
    pack,
    send1,
    recv1,
    qkv,
    send3,
    recv3,
    sendml,
    recvml,
    mscr,
    lscr,
    coefs,
    coef_t,
    att,
    att32,
    x_buf,
    send4,
    recv4,
    fin,
    w_sem,
    wo_sem,
    k_sem,
    v_sem,
    s1_sem,
    r1_sem,
    s2_sem,
    r2_sem,
    s3_sem,
    r3_sem,
    sm_sem,
    rm_sem,
    s5_sem,
    r5_sem,
    s4_sem,
    r4_sem,
    s6_sem,
    r6_sem,
):
    n_seq, n_head, batch, verify, kv_local, heads, ctx_local, col_parts = dims
    draft = verify - 1
    group = heads // kv_local
    per = n_seq // batch
    slots = heads + 2 * kv_local
    qrows = verify * heads
    grows = verify * group
    srows = 2 * qrows
    q_cols = heads * HEAD_DIM
    kv_cols = kv_local * HEAD_DIM
    me = lax.axis_index("seq")
    hd = lax.axis_index("head")
    my_b = me // per
    scale = HEAD_DIM ** (-0.5)

    def on_owner(body):
        if per == 1:
            body()
        else:
            pl.when(lax.rem(me, per) == 0)(body)

    barrier = pltpu.get_barrier_semaphore()
    for off in range(1, n_seq):
        pl.semaphore_signal(
            barrier, inc=1, device_id=(lax.rem(me + off, n_seq), hd), device_id_type=MESH
        )
    for off in range(1, n_head):
        pl.semaphore_signal(
            barrier, inc=1, device_id=(me, lax.rem(hd + off, n_head)), device_id_type=MESH
        )

    step = min(512, q_cols)
    pieces = [(wq, c, step, c) for c in range(0, q_cols, step)]
    pieces += [(wk, 0, kv_cols, q_cols), (wv, 0, kv_cols, q_cols + kv_cols)]
    w_copies = []
    for at, (src, c0, width, d0) in enumerate(pieces):
        copy = pltpu.make_async_copy(
            src.at[:, pl.ds(c0, width)], w_buf.at[:, pl.ds(d0, width)], w_sem.at[at]
        )
        copy.start()
        w_copies.append(copy)

    def cache_copies(b):
        return (
            pltpu.make_async_copy(kc.at[b], k_buf.at[b], k_sem.at[b]),
            pltpu.make_async_copy(vc.at[b], v_buf.at[b], v_sem.at[b]),
        )

    @pl.loop(0, batch)
    def _(i):
        b = lax.rem(my_b + i, batch)
        for copy in cache_copies(b):
            copy.start()

    wo_copy = pltpu.make_async_copy(wo, wo_buf, wo_sem)
    wo_copy.start()

    hs[...] = jnp.zeros_like(hs)
    pack[...] = jnp.zeros_like(pack)
    coefs[...] = jnp.zeros_like(coefs)
    for b in range(batch):
        hs[8 * b : 8 * b + verify, :] = hid[b].astype(F32)
    x_in = hs[...].astype(BF16)
    for copy, (src, c0, width, d0) in zip(w_copies, pieces):
        copy.wait()
        part[:, d0 : d0 + width] = jnp.dot(
            x_in, w_buf[:, d0 : d0 + width], preferred_element_type=F32
        )

    pl.semaphore_wait(barrier, n_seq - 1 + n_head - 1)

    def copy1(b, src):
        return pltpu.make_async_remote_copy(
            src_ref=send1.at[b],
            dst_ref=recv1.at[src],
            send_sem=s1_sem.at[b],
            recv_sem=r1_sem.at[src],
            device_id=(b * per, hd),
            device_id_type=MESH,
        )

    @pl.loop(0, batch)
    def _(i):
        b = lax.rem(my_b + 1 + i, batch)
        row = pl.multiple_of(b * 8, 8)
        for s in range(slots):
            pack[verify * s : verify * s + 8, :] = part[
                pl.ds(row, 8), s * HEAD_DIM : (s + 1) * HEAD_DIM
            ]
        send1[b] = pack[...].astype(BF16)

        @pl.when(b * per != me)
        def _():
            copy1(b, me).start()

    def copy_gather(buf, send_sem, recv_sem, b, dst):
        return pltpu.make_async_remote_copy(
            src_ref=buf.at[b],
            dst_ref=buf.at[b],
            send_sem=send_sem.at[dst],
            recv_sem=recv_sem.at[b],
            device_id=(dst, hd),
            device_id_type=MESH,
        )

    def owner_rotate():
        def add(off, acc):
            src = lax.rem(me + off, n_seq)
            copy1(my_b, src).wait_recv()
            return acc + recv1[src].astype(F32)

        total = lax.fori_loop(1, n_seq, add, send1[my_b].astype(F32))
        shape = total.shape
        row = lax.broadcasted_iota(jnp.int32, shape, 0)
        lane = lax.broadcasted_iota(jnp.int32, shape, 1)
        slot = lax.div(row, verify)
        pos = (ctx[my_b] + (row - slot * verify)).astype(F32)
        angle = pos * inv[...]
        turned = slot < heads + kv_local
        cosine = jnp.where(turned, jnp.cos(angle), 1.0)
        sine = jnp.where(turned, jnp.sin(angle), 0.0)
        sine = jnp.where(lane < HEAD_DIM // 2, -sine, sine)
        qkv[my_b] = (total * cosine + pltpu.roll(total, HEAD_DIM // 2, 1) * sine).astype(BF16)

        @pl.loop(1, n_seq)
        def _(off):
            copy_gather(qkv, s2_sem, r2_sem, my_b, lax.rem(me + off, n_seq)).start()

    on_owner(owner_rotate)

    def statistics(peak, total):
        lane = lax.broadcasted_iota(jnp.int32, (srows, HEAD_DIM), 1)
        wide = jnp.where(lane == 0, peak, jnp.where(lane == 1, total, 0.0))
        extra = sendml.shape[2] - srows
        if extra:
            wide = jnp.concatenate([wide, jnp.zeros((extra, HEAD_DIM), F32)], axis=0)
        return wide.T[0:2, :]

    def softmax(scores, mask):
        masked = jnp.where(mask, scores, NEG)
        peak = jnp.max(masked, axis=1, keepdims=True)
        weights = jnp.where(mask, jnp.exp(masked - peak), 0.0)
        return peak, jnp.sum(weights, axis=1, keepdims=True), weights

    def copy3(b, src):
        return pltpu.make_async_remote_copy(
            src_ref=send3.at[b],
            dst_ref=recv3.at[src],
            send_sem=s3_sem.at[b],
            recv_sem=r3_sem.at[src],
            device_id=(b * per, hd),
            device_id_type=MESH,
        )

    def copyml(b, src):
        return pltpu.make_async_remote_copy(
            src_ref=sendml.at[b],
            dst_ref=recvml.at[src],
            send_sem=sm_sem.at[b],
            recv_sem=rm_sem.at[src],
            device_id=(b * per, hd),
            device_id_type=MESH,
        )

    @pl.loop(0, batch)
    def _(i):
        b = lax.rem(my_b + i, batch)

        @pl.when(b * per != me)
        def _():
            copy_gather(qkv, s2_sem, r2_sem, b, me).wait_recv()

        for copy in cache_copies(b):
            copy.wait()
        query = qkv[b].astype(F32)[0:qrows]
        row = lax.broadcasted_iota(jnp.int32, query.shape, 0)
        spread = jnp.concatenate(
            [
                jnp.where((row >= kv * grows) & (row < (kv + 1) * grows), query, 0.0)
                for kv in range(kv_local)
            ],
            axis=1,
        ).astype(BF16)
        scores = (
            lax.dot_general(
                spread, k_buf[b], (((1,), (1,)), ((), ())), preferred_element_type=F32
            )
            * scale
        )
        lane = lax.broadcasted_iota(jnp.int32, (1, ctx_local), 1)
        live = lane + me * ctx_local < ctx[b]
        flags = jnp.concatenate(
            [
                jnp.full((1, BLOCK), keep[b, blk], jnp.int32)
                for blk in range(ctx_local // BLOCK)
            ],
            axis=1,
        )
        kept = live & (flags > 0)
        t_peak, t_total, t_weights = softmax(scores, live)
        d_peak, d_total, d_weights = softmax(scores, kept)
        weights = jnp.concatenate([t_weights, d_weights], axis=0).astype(BF16)
        values = jnp.dot(weights, v_buf[b], preferred_element_type=F32)
        blocks = []
        for half in range(2):
            for kv in range(kv_local):
                r0 = half * qrows + kv * grows
                blocks.append(values[r0 : r0 + grows, kv * HEAD_DIM : (kv + 1) * HEAD_DIM])
        send3[b] = jnp.concatenate(blocks, axis=0).astype(BF16)
        sendml[b] = statistics(
            jnp.concatenate([t_peak, d_peak], axis=0),
            jnp.concatenate([t_total, d_total], axis=0),
        )

        @pl.when(b * per != me)
        def _():
            copy3(b, me).start()
            copyml(b, me).start()

    def owner_merge():
        rows_all = qkv[my_b].astype(F32)
        query = rows_all[0:qrows]
        raw = lax.dot_general(
            query.astype(BF16), qkv[my_b], (((1,), (1,)), ((), ())), preferred_element_type=F32
        )
        scores = raw * scale
        row = lax.broadcasted_iota(jnp.int32, scores.shape, 0)
        col = lax.broadcasted_iota(jnp.int32, scores.shape, 1) - qrows
        row_head = lax.div(row, verify)
        row_j = row - row_head * verify
        row_kv = lax.div(row_head, group)
        first = row_kv * verify
        mask = (col >= first) & (col <= first + row_j)
        peak, total, weights = softmax(scores, mask)
        weights = weights.astype(BF16)
        vrow = lax.broadcasted_iota(jnp.int32, rows_all.shape, 0) - qrows
        shift = kv_local * verify
        moved = pltpu.roll(rows_all, rows_all.shape[0] - shift, 0)
        moved = jnp.where((vrow >= 0) & (vrow < shift), moved, 0.0).astype(BF16)
        values = jnp.dot(weights, moved, preferred_element_type=F32)
        recv3[n_seq] = jnp.concatenate([values, values], axis=0).astype(BF16)
        recvml[n_seq] = statistics(
            jnp.concatenate([peak, peak], axis=0), jnp.concatenate([total, total], axis=0)
        )
        recv3[me] = send3[my_b]
        recvml[me] = sendml[my_b]

        @pl.loop(1, n_seq)
        def _(off):
            src = lax.rem(me + off, n_seq)
            copyml(my_b, src).wait_recv()
            copy3(my_b, src).wait_recv()

        for s in range(n_seq + 1):
            both = recvml[s]
            mscr[s : s + 1, :] = both[0:1]
            lscr[s : s + 1, :] = both[1:2]
        m_all = mscr[0 : n_seq + 1, :]
        l_all = lscr[0 : n_seq + 1, :]
        factor = jnp.exp(m_all - jnp.max(m_all, axis=0, keepdims=True))
        norm = jnp.sum(factor * l_all, axis=0, keepdims=True)
        norm = jnp.where(norm > 0.0, norm, 1.0)
        coefs[0 : n_seq + 1, :] = factor / norm
        coef_t[...] = coefs[...].T
        acc = jnp.zeros((srows, HEAD_DIM), F32)
        for s in range(n_seq + 1):
            acc = acc + coef_t[0:srows, s : s + 1] * recv3[s].astype(F32)
        att[my_b] = acc.astype(BF16)

        @pl.loop(1, n_seq)
        def _(off):
            copy_gather(att, s5_sem, r5_sem, my_b, lax.rem(me + off, n_seq)).start()

    on_owner(owner_merge)

    @pl.loop(0, batch)
    def _(i):
        b = lax.rem(my_b + i, batch)

        @pl.when(b * per != me)
        def _():
            copy_gather(att, s5_sem, r5_sem, b, me).wait_recv()

        att32[pl.ds(pl.multiple_of(b * srows, 8), srows), :] = att[b].astype(F32)

    planes = [j for j in range(verify)] + [qrows + j for j in range(draft)]
    for pair in range(x_buf.shape[0] // 16):
        for h in range(heads):
            halves = []
            for at in (2 * pair, 2 * pair + 1):
                if at < len(planes):
                    halves.append(
                        att32[pl.ds(planes[at] + h * verify, batch, stride=srows), :]
                    )
                else:
                    halves.append(jnp.zeros((batch, HEAD_DIM), F32))
            x_buf[16 * pair : 16 * pair + 16, h * HEAD_DIM : (h + 1) * HEAD_DIM] = (
                jnp.concatenate(halves, axis=0).astype(BF16)
            )

    part_rows, part_cols = send4.shape[1:]

    def place(at):
        return (at // col_parts) * part_rows, (at % col_parts) * part_cols

    def copy4(at, src):
        return pltpu.make_async_remote_copy(
            src_ref=send4.at[at],
            dst_ref=recv4.at[src],
            send_sem=s4_sem.at[at],
            recv_sem=r4_sem.at[src],
            device_id=(me, at),
            device_id_type=MESH,
        )

    wo_copy.wait()
    for at in range(n_head):
        r0, c0 = place(at)
        send4[at] = jnp.dot(
            x_buf[r0 : r0 + part_rows, :],
            wo_buf[:, c0 : c0 + part_cols],
            preferred_element_type=F32,
        ).astype(BF16)

        @pl.when(hd != at)
        def _():
            copy4(at, hd).start()

    def add_head(off, acc):
        src = lax.rem(hd + off, n_head)
        copy4(hd, src).wait_recv()
        return acc + recv4[src].astype(F32)

    fin[hd] = lax.fori_loop(1, n_head, add_head, send4[hd].astype(F32)).astype(BF16)

    def copy6(at, dst):
        return pltpu.make_async_remote_copy(
            src_ref=fin.at[at],
            dst_ref=fin.at[at],
            send_sem=s6_sem.at[dst],
            recv_sem=r6_sem.at[at],
            device_id=(me, dst),
            device_id_type=MESH,
        )

    @pl.loop(1, n_head)
    def _(off):
        copy6(hd, lax.rem(hd + off, n_head)).start()

    @pl.loop(1, n_head)
    def _(off):
        copy6(lax.rem(hd + off, n_head), hd).wait_recv()

    for at in range(n_head):
        r0, c0 = place(at)
        out[r0 : r0 + part_rows, c0 : c0 + part_cols] = fin[at]

    @pl.loop(0, batch)
    def _(b):
        @pl.when(b * per != me)
        def _():
            copy1(b, me).wait_send()
            copy3(b, me).wait_send()
            copyml(b, me).wait_send()

    def owner_sent():
        @pl.loop(1, n_seq)
        def _(off):
            dst = lax.rem(me + off, n_seq)
            copy_gather(qkv, s2_sem, r2_sem, my_b, dst).wait_send()
            copy_gather(att, s5_sem, r5_sem, my_b, dst).wait_send()

    on_owner(owner_sent)

    @pl.loop(1, n_head)
    def _(off):
        dst = lax.rem(hd + off, n_head)
        copy4(dst, hd).wait_send()
        copy6(hd, dst).wait_send()


def per_device(
    n_seq,
    n_head,
    hidden_states,
    w_query,
    w_key,
    w_value,
    w_out,
    key_cache,
    value_cache,
    context_lengths,
    keep_blocks,
):
    batch, verify, width = hidden_states.shape
    draft = verify - 1
    ctx_local = key_cache.shape[1]
    kv_cols = key_cache.shape[2]
    kv_local = kv_cols // HEAD_DIM
    q_cols = w_query.shape[1]
    heads = q_cols // HEAD_DIM
    out_cols = w_out.shape[1]
    slots = heads + 2 * kv_local
    rows1 = round_up(verify * slots, 16)
    srows = 2 * verify * heads
    lanes = round_up(srows, HEAD_DIM)
    n_rows = batch * (verify + draft)
    col_parts = math.gcd(n_head, out_cols // HEAD_DIM)
    row_parts = n_head // col_parts
    part_rows = round_up(-(-n_rows // row_parts), 16)
    part_cols = out_cols // col_parts
    all_rows = part_rows * row_parts
    src_rows = round_up(n_seq + 1, 8)
    dims = (n_seq, n_head, batch, verify, kv_local, heads, ctx_local, col_parts)

    inverse = (500000.0 ** (-(np.arange(HEAD_DIM // 2) * 2.0) / HEAD_DIM)).astype(np.float32)
    inverse = jnp.asarray(np.concatenate([inverse, inverse])[None, :])

    vmem = pl.BlockSpec(memory_space=pltpu.VMEM)
    smem = pl.BlockSpec(memory_space=pltpu.SMEM)
    hbm = pl.BlockSpec(memory_space=pl.ANY)
    dma = pltpu.SemaphoreType.DMA
    result = pl.pallas_call(
        functools.partial(kernel, dims),
        out_shape=jax.ShapeDtypeStruct((all_rows, out_cols), BF16),
        in_specs=[vmem, vmem, smem, smem] + [hbm] * 6,
        out_specs=vmem,
        scratch_shapes=[
            pltpu.VMEM((width, q_cols + 2 * kv_cols), BF16),
            pltpu.VMEM(w_out.shape, BF16),
            pltpu.VMEM(key_cache.shape, BF16),
            pltpu.VMEM(value_cache.shape, BF16),
            pltpu.VMEM((8 * batch, width), F32),
            pltpu.VMEM((8 * batch, q_cols + 2 * kv_cols), F32),
            pltpu.VMEM((rows1, HEAD_DIM), F32),
            pltpu.VMEM((batch, rows1, HEAD_DIM), BF16),
            pltpu.VMEM((n_seq, rows1, HEAD_DIM), BF16),
            pltpu.VMEM((batch, rows1, HEAD_DIM), BF16),
            pltpu.VMEM((batch, srows, HEAD_DIM), BF16),
            pltpu.VMEM((n_seq + 1, srows, HEAD_DIM), BF16),
            pltpu.VMEM((batch, 2, lanes), F32),
            pltpu.VMEM((n_seq + 1, 2, lanes), F32),
            pltpu.VMEM((src_rows, lanes), F32),
            pltpu.VMEM((src_rows, lanes), F32),
            pltpu.VMEM((HEAD_DIM, lanes), F32),
            pltpu.VMEM((lanes, HEAD_DIM), F32),
            pltpu.VMEM((batch, srows, HEAD_DIM), BF16),
            pltpu.VMEM((batch * srows, HEAD_DIM), F32),
            pltpu.VMEM((all_rows, q_cols), BF16),
            pltpu.VMEM((n_head, part_rows, part_cols), BF16),
            pltpu.VMEM((n_head, part_rows, part_cols), BF16),
            pltpu.VMEM((n_head, part_rows, part_cols), BF16),
            dma((q_cols // min(512, q_cols) + 2,)),
            dma,
            dma((batch,)),
            dma((batch,)),
            dma((batch,)),
            dma((n_seq,)),
            dma((n_seq,)),
            dma((batch,)),
            dma((batch,)),
            dma((n_seq,)),
            dma((batch,)),
            dma((n_seq,)),
            dma((n_seq,)),
            dma((batch,)),
            dma((n_head,)),
            dma((n_head,)),
            dma((n_head,)),
            dma((n_head,)),
        ],
        compiler_params=pltpu.CompilerParams(
            collective_id=0, has_side_effects=True, vmem_limit_bytes=56 * 1024 * 1024
        ),
        name="verify_round",
    )(
        hidden_states,
        inverse,
        context_lengths,
        keep_blocks,
        w_query,
        w_key,
        w_value,
        w_out,
        key_cache,
        value_cache,
    )
    target_rows = batch * verify
    verify_out = result[:target_rows].reshape(verify, batch, out_cols).transpose(1, 0, 2)
    draft_out = result[target_rows:n_rows].reshape(draft, batch, out_cols).transpose(1, 0, 2)
    return verify_out, draft_out


def solution(mesh):
    placed = (
        P(None, None, "seq"),
        P("seq", "head"),
        P("seq", "head"),
        P("seq", "head"),
        P("head", "seq"),
        P(None, "seq", "head"),
        P(None, "seq", "head"),
        P(),
        P(None, "seq"),
    )
    return jax.shard_map(
        functools.partial(per_device, mesh.shape["seq"], mesh.shape["head"]),
        mesh=mesh,
        in_specs=placed,
        out_specs=(P(None, None, "seq"), P(None, None, "seq")),
        check_vma=False,
    )
```

time: 305 us -> 49.4 us (0.16)
  waiting for transfers between devices: 156 us -> 0 us
  blocking collectives: 73.6 us -> 0 us
  Pallas kernels: 0 us -> 43.9 us
  matrix products: 20.9 us -> 0 us
  local copies, waits for them, and re-layouts: 23 us -> 4.64 us
  other arithmetic: 16.2 us -> 0 us
  between operations: 14 us -> 0.64 us
    psum x3 -> x0, waiting for transfers between devices: 156 us -> none  [the longest x1 69.1 us: per_device(): lax.psum((target_total * factor_target, target_weighted * factor_target[....]
    pallas_call x0 -> x1, Pallas kernels: none -> 43.9 us  [per_device(): pl.pallas_call(functools.partial(kernel, dims), out_shape=jax.ShapeDtypeS...]
    pmax x1 -> x0, blocking collectives: 36.8 us -> none  [per_device(): peak_target, peak_draft = lax.pmax((target_peak, draft_peak), 'seq')]
    psum x1 -> x0, blocking collectives: 36.7 us -> none  [per_device(): lax.psum((query_part, key_part, value_part), 'seq')]
    dot_general x10 -> x0, matrix products: 20.9 us -> none  [the longest x2 5.91 us: partial_softmax(): jnp.einsum('bkjgt,btkd->bkjgd', weights.astype(jnp.bfloat16), cache_value...]
    reshape x9 -> x2, local copies, waits for them, and re-layouts: 15.4 us -> 1.53 us  [per_device(): result[target_rows:n_rows].reshape(draft, batch, out_cols)]
    reduce_sum x4 -> x0, other arithmetic: 5.52 us -> none  [the longest x2 2.88 us: finish(): total_sum = total_sum * factor_old + jnp.sum(weights, axis=-1)]
  transfers between devices with their start and end apart: 3 -> 0, of which waited for: 3 -> 0; matrix products, arithmetic and copies ran while one was open for 6% -> 0% of each run, Pallas kernels for 0% -> 0%
where the time goes in v1:
time: 49.4 us; the launch traced here: 49.2 us
  Pallas kernels  43.9 us (89%)
  local copies, waits for them, and re-layouts  4.64 us (9%)
  between operations  0.64 us (1%)
    pallas_call x1, Pallas kernels, per_device(): pl.pallas_call(functools.partial(kernel, dims), out_shape=jax.ShapeDtypeS...  43.9 us
    unnamed x1, local copies, waits for them, and re-layouts  1.58 us
    reshape x2, local copies, waits for them, and re-layouts, per_device(): result[target_rows:n_rows].reshape(draft, batch, out_cols)  1.53 us
    transpose x1, local copies, waits for them, and re-layouts, per_device(): result[:target_rows].reshape(verify, batch, out_cols).transpose(1, 0, 2)  1.53 us

profile of v1, /device:TPU:0, one launch (start us, length us, event | category | flops | bytes accessed | tf_op | source)
XLA Modules:
  0.0 49.2 jit_solution(14709186217378905909)
XLA Ops:
  0.6 1.6 %copy.12.hid = bf16[8,5,1024]{2,1,0:T(8,128)(2,1)} copy(bf16[8,5,1024]{2,0,1:T(8,128)(2,1)} %param.10) | data formatting | bytes 163840 | tf_op args[0]
  2.2 43.9 %verify_round.1 = bf16[80,1024]{1,0:T(8,128)(2,1)} custom-call(bf16[8,5,1024]{2,1,0:T(8,128)(2,1)} %copy.12.hid, f32[1,128]{1,0:T(1,128)} %constant.2.clone.inv, s32[8]{0:T(128)} %ctx.1, s32[8,8]{1,0:T(8,128)} %keep.1, bf16[1024,2048]{1,0:T(8,128)(2,1)} %wq.1, bf16[1024,256]{1,0:T(8,128)(2,1)} %wk.1, bf16[1024,256]{1,0:T(8,128)(2,1)} %wv.1, ...), custom_call_target="tpu_custom_call" | custom-call | tf_op jit(solution)/shard_map/verify_round/pallas_call | solution.py:502
  46.1 0.8 %slice_bitcast_fusion.1 = bf16[4,8,1024]{2,1,0:T(8,128)(2,1)S(1)} fusion(bf16[80,1024]{1,0:T(8,128)(2,1)} %verify_round.1), kind=kLoop, calls=%fused_computation.2 | loop fusion | bytes 131072 | tf_op jit(solution)/shard_map/reshape | solution.py:569
  46.9 1.5 %slice_bitcast_fusion = bf16[8,5,1024]{2,0,1:T(8,128)(2,1)} fusion(bf16[80,1024]{1,0:T(8,128)(2,1)} %verify_round.1), kind=kLoop, calls=%fused_computation | loop fusion | bytes 163840 | tf_op jit(solution)/shard_map/transpose | solution.py:568
  48.5 0.7 %copy.15 = bf16[4,8,1024]{2,0,1:T(4,128)(2,1)} copy(bf16[4,8,1024]{2,1,0:T(8,128)(2,1)S(1)} %slice_bitcast_fusion.1) | data formatting | bytes 131072 | tf_op jit(solution)/shard_map/reshape | solution.py:569

commit v2 on v1

--- a/solution.py
+++ b/solution.py
@@ -33,21 +33,24 @@
     wo,
     kc,
     vc,
-    out,
+    out_v,
+    out_d,
     w_buf,
     wo_buf,
     k_buf,
     v_buf,
-    hs,
-    part,
     pack,
     send1,
     recv1,
     qkv,
+    query_all,
     send3,
     recv3,
+    pair3,
     sendml,
     recvml,
+    pairml,
+    pairs,
     mscr,
     lscr,
     coefs,
@@ -58,6 +61,7 @@
     send4,
     recv4,
     fin,
+    y32,
     w_sem,
     wo_sem,
     k_sem,
@@ -68,10 +72,13 @@
     r2_sem,
     s3_sem,
     r3_sem,
+    p3_sem,
     sm_sem,
     rm_sem,
+    pm_sem,
     s5_sem,
     r5_sem,
+    f5_sem,
     s4_sem,
     r4_sem,
     s6_sem,
@@ -90,7 +97,28 @@
     me = lax.axis_index("seq")
     hd = lax.axis_index("head")
     my_b = me // per
-    scale = HEAD_DIM ** (-0.5)
+    scale = HEAD_DIM ** (-0.5) * math.log2(math.e)
+    rows1 = send1.shape[1]
+    lines = n_seq // 2
+    line, side = me // 2, lax.rem(me, 2)
+    partner = me + 1 - 2 * side
+
+    def use_order(i):
+        if per > 1:
+            return lax.rem(my_b + i, batch)
+        other = jnp.where((i >= 1) & (i <= lines), 1 - side, side)
+        return 2 * lax.rem(line + i, lines) + other
+
+    def gather_order(i):
+        if per > 1:
+            return lax.rem(my_b + i, batch)
+        return 2 * lax.rem(line + i, lines) + jnp.where(i < lines, side, 1 - side)
+
+    def is_mine(b):
+        return lax.rem(b * per, 2) == side
+
+    def is_own(b):
+        return b * per == me
 
     def on_owner(body):
         if per == 1:
@@ -125,26 +153,27 @@
             pltpu.make_async_copy(vc.at[b], v_buf.at[b], v_sem.at[b]),
         )
 
+    pack[...] = jnp.zeros_like(pack)
+    coefs[...] = jnp.zeros_like(coefs)
+    pairs[...] = jnp.zeros_like(pairs)
+    x_in = hid[...]
+    for copy, (src, c0, width, d0) in zip(w_copies, pieces):
+        copy.wait()
+        piece = jnp.dot(x_in, w_buf[:, d0 : d0 + width], preferred_element_type=F32)
+        for s in range(width // HEAD_DIM):
+            slot = d0 // HEAD_DIM + s
+            for j in range(verify):
+                pack[pl.ds(slot * verify + j, batch, stride=rows1), :] = piece[
+                    j * batch : (j + 1) * batch, s * HEAD_DIM : (s + 1) * HEAD_DIM
+                ]
+
     @pl.loop(0, batch)
     def _(i):
-        b = lax.rem(my_b + i, batch)
-        for copy in cache_copies(b):
+        for copy in cache_copies(use_order(i)):
             copy.start()
 
     wo_copy = pltpu.make_async_copy(wo, wo_buf, wo_sem)
     wo_copy.start()
-
-    hs[...] = jnp.zeros_like(hs)
-    pack[...] = jnp.zeros_like(pack)
-    coefs[...] = jnp.zeros_like(coefs)
-    for b in range(batch):
-        hs[8 * b : 8 * b + verify, :] = hid[b].astype(F32)
-    x_in = hs[...].astype(BF16)
-    for copy, (src, c0, width, d0) in zip(w_copies, pieces):
-        copy.wait()
-        part[:, d0 : d0 + width] = jnp.dot(
-            x_in, w_buf[:, d0 : d0 + width], preferred_element_type=F32
-        )
 
     pl.semaphore_wait(barrier, n_seq - 1 + n_head - 1)
 
@@ -161,12 +190,7 @@
     @pl.loop(0, batch)
     def _(i):
         b = lax.rem(my_b + 1 + i, batch)
-        row = pl.multiple_of(b * 8, 8)
-        for s in range(slots):
-            pack[verify * s : verify * s + 8, :] = part[
-                pl.ds(row, 8), s * HEAD_DIM : (s + 1) * HEAD_DIM
-            ]
-        send1[b] = pack[...].astype(BF16)
+        send1[b] = pack[pl.ds(pl.multiple_of(b * rows1, 16), rows1), :].astype(BF16)
 
         @pl.when(b * per != me)
         def _():
@@ -199,11 +223,18 @@
         cosine = jnp.where(turned, jnp.cos(angle), 1.0)
         sine = jnp.where(turned, jnp.sin(angle), 0.0)
         sine = jnp.where(lane < HEAD_DIM // 2, -sine, sine)
-        qkv[my_b] = (total * cosine + pltpu.roll(total, HEAD_DIM // 2, 1) * sine).astype(BF16)
+        turned = total * cosine + pltpu.roll(total, HEAD_DIM // 2, 1) * sine
+        qkv[...] = turned.astype(BF16)
+        query_all[my_b] = turned[0 : query_all.shape[1]].astype(BF16)
 
         @pl.loop(1, n_seq)
         def _(off):
-            copy_gather(qkv, s2_sem, r2_sem, my_b, lax.rem(me + off, n_seq)).start()
+            if per > 1:
+                dst = lax.rem(me + off, n_seq)
+            else:
+                other = jnp.where(off <= lines, 1 - side, side)
+                dst = 2 * lax.rem(line + n_seq - off, lines) + other
+            copy_gather(query_all, s2_sem, r2_sem, my_b, dst).start()
 
     on_owner(owner_rotate)
 
@@ -217,41 +248,53 @@
 
     def softmax(scores, mask):
         masked = jnp.where(mask, scores, NEG)
-        peak = jnp.max(masked, axis=1, keepdims=True)
-        weights = jnp.where(mask, jnp.exp(masked - peak), 0.0)
+        peak = jnp.maximum(jnp.max(masked, axis=1, keepdims=True), NEG / 8)
+        weights = jnp.exp2(masked - peak)
         return peak, jnp.sum(weights, axis=1, keepdims=True), weights
 
-    def copy3(b, src):
-        return pltpu.make_async_remote_copy(
-            src_ref=send3.at[b],
-            dst_ref=recv3.at[src],
-            send_sem=s3_sem.at[b],
-            recv_sem=r3_sem.at[src],
-            device_id=(b * per, hd),
-            device_id_type=MESH,
-        )
-
-    def copyml(b, src):
-        return pltpu.make_async_remote_copy(
-            src_ref=sendml.at[b],
-            dst_ref=recvml.at[src],
-            send_sem=sm_sem.at[b],
-            recv_sem=rm_sem.at[src],
-            device_id=(b * per, hd),
-            device_id_type=MESH,
-        )
+    def copies_up(b, src):
+        return [
+            pltpu.make_async_remote_copy(
+                src_ref=source.at[b],
+                dst_ref=target.at[src // 2],
+                send_sem=send_sem.at[b],
+                recv_sem=recv_sem.at[src // 2],
+                device_id=(b * per, hd),
+                device_id_type=MESH,
+            )
+            for source, target, send_sem, recv_sem in (
+                (sendml, recvml, sm_sem, rm_sem),
+                (send3, recv3, s3_sem, r3_sem),
+            )
+        ]
+
+    def copies_across(b):
+        return [
+            pltpu.make_async_remote_copy(
+                src_ref=source.at[b],
+                dst_ref=target.at[b],
+                send_sem=send_sem.at[b],
+                recv_sem=recv_sem.at[b],
+                device_id=(partner, hd),
+                device_id_type=MESH,
+            )
+            for source, target, send_sem, recv_sem in (
+                (sendml, pairml, sm_sem, pm_sem),
+                (send3, pair3, s3_sem, p3_sem),
+            )
+        ]
 
     @pl.loop(0, batch)
     def _(i):
-        b = lax.rem(my_b + i, batch)
+        b = use_order(i)
 
         @pl.when(b * per != me)
         def _():
-            copy_gather(qkv, s2_sem, r2_sem, b, me).wait_recv()
+            copy_gather(query_all, s2_sem, r2_sem, b, me).wait_recv()
 
         for copy in cache_copies(b):
             copy.wait()
-        query = qkv[b].astype(F32)[0:qrows]
+        query = query_all[b].astype(F32)[0:qrows]
         row = lax.broadcasted_iota(jnp.int32, query.shape, 0)
         spread = jnp.concatenate(
             [
@@ -285,22 +328,42 @@
             for kv in range(kv_local):
                 r0 = half * qrows + kv * grows
                 blocks.append(values[r0 : r0 + grows, kv * HEAD_DIM : (kv + 1) * HEAD_DIM])
-        send3[b] = jnp.concatenate(blocks, axis=0).astype(BF16)
-        sendml[b] = statistics(
-            jnp.concatenate([t_peak, d_peak], axis=0),
-            jnp.concatenate([t_total, d_total], axis=0),
-        )
-
-        @pl.when(b * per != me)
-        def _():
-            copy3(b, me).start()
-            copyml(b, me).start()
+        values = jnp.concatenate(blocks, axis=0)
+        peak = jnp.concatenate([t_peak, d_peak], axis=0)
+        total = jnp.concatenate([t_total, d_total], axis=0)
+
+        @pl.when(is_own(b))
+        def _():
+            recv3[line] = values.astype(BF16)
+            recvml[line] = statistics(peak, total)
+
+        @pl.when(jnp.logical_not(is_mine(b)))
+        def _():
+            send3[b] = values.astype(BF16)
+            sendml[b] = statistics(peak, total)
+            for copy in copies_across(b):
+                copy.start()
+
+        @pl.when(is_mine(b) & jnp.logical_not(is_own(b)))
+        def _():
+            for copy in copies_across(b):
+                copy.wait_recv()
+            pairs[0:2, :] = pairml[b]
+            theirs = pairs[...].T
+            their_peak = theirs[0:srows, 0:1]
+            joint = jnp.maximum(peak, their_peak)
+            ours = jnp.exp2(peak - joint)
+            other = jnp.exp2(their_peak - joint)
+            send3[b] = (values * ours + pair3[b].astype(F32) * other).astype(BF16)
+            sendml[b] = statistics(joint, total * ours + theirs[0:srows, 1:2] * other)
+            for copy in copies_up(b, me):
+                copy.start()
 
     def owner_merge():
-        rows_all = qkv[my_b].astype(F32)
+        rows_all = qkv[...].astype(F32)
         query = rows_all[0:qrows]
         raw = lax.dot_general(
-            query.astype(BF16), qkv[my_b], (((1,), (1,)), ((), ())), preferred_element_type=F32
+            query.astype(BF16), qkv[...], (((1,), (1,)), ((), ())), preferred_element_type=F32
         )
         scores = raw * scale
         row = lax.broadcasted_iota(jnp.int32, scores.shape, 0)
@@ -317,48 +380,68 @@
         moved = pltpu.roll(rows_all, rows_all.shape[0] - shift, 0)
         moved = jnp.where((vrow >= 0) & (vrow < shift), moved, 0.0).astype(BF16)
         values = jnp.dot(weights, moved, preferred_element_type=F32)
-        recv3[n_seq] = jnp.concatenate([values, values], axis=0).astype(BF16)
-        recvml[n_seq] = statistics(
+        fresh = lines + 1
+        recv3[fresh] = jnp.concatenate([values, values], axis=0).astype(BF16)
+        recvml[fresh] = statistics(
             jnp.concatenate([peak, peak], axis=0), jnp.concatenate([total, total], axis=0)
         )
-        recv3[me] = send3[my_b]
-        recvml[me] = sendml[my_b]
-
-        @pl.loop(1, n_seq)
+        for copy in copies_across(my_b):
+            copy.wait_recv()
+        recv3[lines] = pair3[my_b]
+        recvml[lines] = pairml[my_b]
+
+        @pl.loop(1, lines)
         def _(off):
-            src = lax.rem(me + off, n_seq)
-            copyml(my_b, src).wait_recv()
-            copy3(my_b, src).wait_recv()
-
-        for s in range(n_seq + 1):
+            for copy in copies_up(my_b, 2 * lax.rem(line + off, lines)):
+                copy.wait_recv()
+
+        n_src = lines + 2
+        for s in range(n_src):
             both = recvml[s]
             mscr[s : s + 1, :] = both[0:1]
             lscr[s : s + 1, :] = both[1:2]
-        m_all = mscr[0 : n_seq + 1, :]
-        l_all = lscr[0 : n_seq + 1, :]
-        factor = jnp.exp(m_all - jnp.max(m_all, axis=0, keepdims=True))
+        m_all = mscr[0:n_src, :]
+        l_all = lscr[0:n_src, :]
+        factor = jnp.exp2(m_all - jnp.max(m_all, axis=0, keepdims=True))
         norm = jnp.sum(factor * l_all, axis=0, keepdims=True)
         norm = jnp.where(norm > 0.0, norm, 1.0)
-        coefs[0 : n_seq + 1, :] = factor / norm
+        coefs[0:n_src, :] = factor / norm
         coef_t[...] = coefs[...].T
         acc = jnp.zeros((srows, HEAD_DIM), F32)
-        for s in range(n_seq + 1):
+        for s in range(n_src):
             acc = acc + coef_t[0:srows, s : s + 1] * recv3[s].astype(F32)
         att[my_b] = acc.astype(BF16)
 
-        @pl.loop(1, n_seq)
+        copy_gather(att, s5_sem, r5_sem, my_b, partner).start()
+
+        @pl.loop(1, lines)
         def _(off):
-            copy_gather(att, s5_sem, r5_sem, my_b, lax.rem(me + off, n_seq)).start()
+            dst = 2 * lax.rem(line + off, lines) + side
+            copy_gather(att, s5_sem, r5_sem, my_b, dst).start()
 
     on_owner(owner_merge)
+
+    def copy_forward(b):
+        return pltpu.make_async_remote_copy(
+            src_ref=att.at[b],
+            dst_ref=att.at[b],
+            send_sem=f5_sem.at[b],
+            recv_sem=r5_sem.at[b],
+            device_id=(partner, hd),
+            device_id_type=MESH,
+        )
 
     @pl.loop(0, batch)
     def _(i):
-        b = lax.rem(my_b + i, batch)
-
-        @pl.when(b * per != me)
-        def _():
-            copy_gather(att, s5_sem, r5_sem, b, me).wait_recv()
+        b = gather_order(i)
+
+        @pl.when(jnp.logical_not(is_own(b)))
+        def _():
+            copy_forward(b).wait_recv()
+
+        @pl.when(is_mine(b) & jnp.logical_not(is_own(b)))
+        def _():
+            copy_forward(b).start()
 
         att32[pl.ds(pl.multiple_of(b * srows, 8), srows), :] = att[b].astype(F32)
 
@@ -378,6 +461,7 @@
             )
 
     part_rows, part_cols = send4.shape[1:]
+    all_rows = x_buf.shape[0]
 
     def place(at):
         return (at // col_parts) * part_rows, (at % col_parts) * part_cols
@@ -432,22 +516,47 @@
 
     for at in range(n_head):
         r0, c0 = place(at)
-        out[r0 : r0 + part_rows, c0 : c0 + part_cols] = fin[at]
+        for c in range(part_cols // HEAD_DIM):
+            base = (c0 // HEAD_DIM + c) * all_rows + r0
+            y32[base : base + part_rows, :] = fin[
+                at, :, c * HEAD_DIM : (c + 1) * HEAD_DIM
+            ].astype(F32)
+    target_rows = verify * batch
+    chunks = range(out_v.shape[1] // HEAD_DIM)
+    for c in chunks:
+        out_v[:, c * HEAD_DIM : (c + 1) * HEAD_DIM] = y32[
+            c * all_rows : c * all_rows + target_rows, :
+        ].astype(BF16)
+    for b in range(batch):
+        out_d[b] = jnp.concatenate(
+            [
+                y32[pl.ds(c * all_rows + target_rows + b, draft, stride=batch), :]
+                for c in chunks
+            ],
+            axis=1,
+        ).astype(BF16)
 
     @pl.loop(0, batch)
     def _(b):
         @pl.when(b * per != me)
         def _():
             copy1(b, me).wait_send()
-            copy3(b, me).wait_send()
-            copyml(b, me).wait_send()
+            for copy in copies_up(b, me):
+                copy.wait_send()
+
+        @pl.when(is_mine(b) & jnp.logical_not(is_own(b)))
+        def _():
+            copy_forward(b).wait_send()
 
     def owner_sent():
         @pl.loop(1, n_seq)
         def _(off):
             dst = lax.rem(me + off, n_seq)
-            copy_gather(qkv, s2_sem, r2_sem, my_b, dst).wait_send()
-            copy_gather(att, s5_sem, r5_sem, my_b, dst).wait_send()
+            copy_gather(query_all, s2_sem, r2_sem, my_b, dst).wait_send()
+
+            @pl.when((dst == partner) | (lax.rem(dst, 2) == side))
+            def _():
+                copy_gather(att, s5_sem, r5_sem, my_b, dst).wait_send()
 
     on_owner(owner_sent)
 
@@ -489,7 +598,9 @@
     part_rows = round_up(-(-n_rows // row_parts), 16)
     part_cols = out_cols // col_parts
     all_rows = part_rows * row_parts
-    src_rows = round_up(n_seq + 1, 8)
+    n_src = n_seq // 2 + 2
+    src_rows = round_up(n_src, 8)
+    qpad = round_up(verify * heads, 16)
     dims = (n_seq, n_head, batch, verify, kv_local, heads, ctx_local, col_parts)
 
     inverse = (500000.0 ** (-(np.arange(HEAD_DIM // 2) * 2.0) / HEAD_DIM)).astype(np.float32)
@@ -499,26 +610,31 @@
     smem = pl.BlockSpec(memory_space=pltpu.SMEM)
     hbm = pl.BlockSpec(memory_space=pl.ANY)
     dma = pltpu.SemaphoreType.DMA
-    result = pl.pallas_call(
+    target, drafted = pl.pallas_call(
         functools.partial(kernel, dims),
-        out_shape=jax.ShapeDtypeStruct((all_rows, out_cols), BF16),
+        out_shape=(
+            jax.ShapeDtypeStruct((batch * verify, out_cols), BF16),
+            jax.ShapeDtypeStruct((batch, draft, out_cols), BF16),
+        ),
         in_specs=[vmem, vmem, smem, smem] + [hbm] * 6,
-        out_specs=vmem,
+        out_specs=(vmem, vmem),
         scratch_shapes=[
             pltpu.VMEM((width, q_cols + 2 * kv_cols), BF16),
             pltpu.VMEM(w_out.shape, BF16),
             pltpu.VMEM(key_cache.shape, BF16),
             pltpu.VMEM(value_cache.shape, BF16),
-            pltpu.VMEM((8 * batch, width), F32),
-            pltpu.VMEM((8 * batch, q_cols + 2 * kv_cols), F32),
-            pltpu.VMEM((rows1, HEAD_DIM), F32),
+            pltpu.VMEM((batch * rows1, HEAD_DIM), F32),
             pltpu.VMEM((batch, rows1, HEAD_DIM), BF16),
             pltpu.VMEM((n_seq, rows1, HEAD_DIM), BF16),
-            pltpu.VMEM((batch, rows1, HEAD_DIM), BF16),
+            pltpu.VMEM((rows1, HEAD_DIM), BF16),
+            pltpu.VMEM((batch, qpad, HEAD_DIM), BF16),
             pltpu.VMEM((batch, srows, HEAD_DIM), BF16),
-            pltpu.VMEM((n_seq + 1, srows, HEAD_DIM), BF16),
+            pltpu.VMEM((n_src, srows, HEAD_DIM), BF16),
+            pltpu.VMEM((batch, srows, HEAD_DIM), BF16),
             pltpu.VMEM((batch, 2, lanes), F32),
-            pltpu.VMEM((n_seq + 1, 2, lanes), F32),
+            pltpu.VMEM((n_src, 2, lanes), F32),
+            pltpu.VMEM((batch, 2, lanes), F32),
+            pltpu.VMEM((HEAD_DIM, lanes), F32),
             pltpu.VMEM((src_rows, lanes), F32),
             pltpu.VMEM((src_rows, lanes), F32),
             pltpu.VMEM((HEAD_DIM, lanes), F32),
@@ -529,6 +645,7 @@
             pltpu.VMEM((n_head, part_rows, part_cols), BF16),
             pltpu.VMEM((n_head, part_rows, part_cols), BF16),
             pltpu.VMEM((n_head, part_rows, part_cols), BF16),
+            pltpu.VMEM((out_cols // HEAD_DIM * all_rows, HEAD_DIM), F32),
             dma((q_cols // min(512, q_cols) + 2,)),
             dma,
             dma((batch,)),
@@ -538,10 +655,13 @@
             dma((n_seq,)),
             dma((batch,)),
             dma((batch,)),
+            dma((n_seq // 2,)),
+            dma((batch,)),
+            dma((batch,)),
+            dma((n_seq // 2,)),
+            dma((batch,)),
             dma((n_seq,)),
             dma((batch,)),
-            dma((n_seq,)),
-            dma((n_seq,)),
             dma((batch,)),
             dma((n_head,)),
             dma((n_head,)),
@@ -553,7 +673,7 @@
         ),
         name="verify_round",
     )(
-        hidden_states,
+        hidden_states.transpose(1, 0, 2).reshape(verify * batch, width),
         inverse,
         context_lengths,
         keep_blocks,
@@ -564,10 +684,7 @@
         key_cache,
         value_cache,
     )
-    target_rows = batch * verify
-    verify_out = result[:target_rows].reshape(verify, batch, out_cols).transpose(1, 0, 2)
-    draft_out = result[target_rows:n_rows].reshape(draft, batch, out_cols).transpose(1, 0, 2)
-    return verify_out, draft_out
+    return target.reshape(verify, batch, out_cols).transpose(1, 0, 2), drafted
 
 
 def solution(mesh):

time: 49.4 us -> 50.4 us (1.020)
  Pallas kernels: 43.9 us -> 46.5 us
  local copies, waits for them, and re-layouts: 4.64 us -> 3.02 us
    pallas_call x1, Pallas kernels: 43.9 us -> 46.5 us  [per_device(): pl.pallas_call(functools.partial(kernel, dims), out_shape=(jax.ShapeDtype...]
    reshape x2 -> x0, local copies, waits for them, and re-layouts: 1.53 us -> none  [per_device(): result[target_rows:n_rows].reshape(draft, batch, out_cols)]
    transpose x1 -> x0, local copies, waits for them, and re-layouts: 1.53 us -> none  [per_device(): result[:target_rows].reshape(verify, batch, out_cols).transpose(1, 0, 2)]
    unnamed x1 -> x2, local copies, waits for them, and re-layouts: 1.58 us -> 3.02 us
where the time goes in v2:
time: 50.4 us; the launch traced here: 50.2 us
  Pallas kernels  46.5 us (92%)
  local copies, waits for them, and re-layouts  3.02 us (6%)
  between operations  0.64 us (1%)
    pallas_call x1, Pallas kernels, per_device(): pl.pallas_call(functools.partial(kernel, dims), out_shape=(jax.ShapeDtype...  46.5 us
    unnamed x2, local copies, waits for them, and re-layouts  3.02 us

profile of v2, /device:TPU:0, one launch (start us, length us, event | category | flops | bytes accessed | tf_op | source)
XLA Modules:
  0.0 50.2 jit_solution(11666167695688301802)
XLA Ops:
  0.6 46.5 %verify_round.1 = (bf16[40,1024]{1,0:T(8,128)(2,1)}, bf16[8,4,1024]{2,1,0:T(4,128)(2,1)}) custom-call(bf16[40,1024]{1,0:T(8,128)(2,1)} %bitcast.7, f32[1,128]{1,0:T(1,128)} %constant.2.clone.inv, s32[8]{0:T(128)} %ctx.1, s32[8,8]{1,0:T(8,128)} %keep.1, bf16[1024,2048]{1,0:T(8,128)(2,1)} %wq.1, bf16[1024,256]{1,0:T(8,128)(2,1)} %wk.1, bf16[1024,256]{1,0:T(8,128)(2,1)} %wv.1, ...), custom_call_target="tpu_custom_call" | custom-call | tf_op jit(solution)/shard_map/verify_round/pallas_call | solution.py:613
  47.2 1.5 %copy.14 = bf16[8,5,1024]{2,0,1:T(8,128)(2,1)} copy(bf16[8,5,1024]{2,0,1:T(8,128)(2,1)} %bitcast.6) | data formatting | bytes 163840
  48.7 1.5 %copy.15 = bf16[8,4,1024]{2,1,0:T(4,128)(2,1)} copy(bf16[8,4,1024]{2,1,0:T(4,128)(2,1)} %get-tuple-element.9) | data formatting | bytes 131072

commit v3 on v2

--- a/solution.py
+++ b/solution.py
@@ -46,11 +46,10 @@
     query_all,
     send3,
     recv3,
-    pair3,
     sendml,
     recvml,
-    pairml,
-    pairs,
+    cos_buf,
+    sin_buf,
     mscr,
     lscr,
     coefs,
@@ -72,10 +71,8 @@
     r2_sem,
     s3_sem,
     r3_sem,
-    p3_sem,
     sm_sem,
     rm_sem,
-    pm_sem,
     s5_sem,
     r5_sem,
     f5_sem,
@@ -106,8 +103,7 @@
     def use_order(i):
         if per > 1:
             return lax.rem(my_b + i, batch)
-        other = jnp.where((i >= 1) & (i <= lines), 1 - side, side)
-        return 2 * lax.rem(line + i, lines) + other
+        return 2 * lax.rem(line + i // 2, lines) + lax.rem(side + i, 2)
 
     def gather_order(i):
         if per > 1:
@@ -153,9 +149,22 @@
             pltpu.make_async_copy(vc.at[b], v_buf.at[b], v_sem.at[b]),
         )
 
+    def rotation():
+        shape = cos_buf.shape
+        row = lax.broadcasted_iota(jnp.int32, shape, 0)
+        lane = lax.broadcasted_iota(jnp.int32, shape, 1)
+        slot = lax.div(row, verify)
+        pos = (ctx[my_b] + (row - slot * verify)).astype(F32)
+        angle = pos * inv[...]
+        turned = slot < heads + kv_local
+        sine = jnp.where(turned, jnp.sin(angle), 0.0)
+        cos_buf[...] = jnp.where(turned, jnp.cos(angle), 1.0)
+        sin_buf[...] = jnp.where(lane < HEAD_DIM // 2, -sine, sine)
+
+    on_owner(rotation)
+
     pack[...] = jnp.zeros_like(pack)
     coefs[...] = jnp.zeros_like(coefs)
-    pairs[...] = jnp.zeros_like(pairs)
     x_in = hid[...]
     for copy, (src, c0, width, d0) in zip(w_copies, pieces):
         copy.wait()
@@ -213,17 +222,7 @@
             return acc + recv1[src].astype(F32)
 
         total = lax.fori_loop(1, n_seq, add, send1[my_b].astype(F32))
-        shape = total.shape
-        row = lax.broadcasted_iota(jnp.int32, shape, 0)
-        lane = lax.broadcasted_iota(jnp.int32, shape, 1)
-        slot = lax.div(row, verify)
-        pos = (ctx[my_b] + (row - slot * verify)).astype(F32)
-        angle = pos * inv[...]
-        turned = slot < heads + kv_local
-        cosine = jnp.where(turned, jnp.cos(angle), 1.0)
-        sine = jnp.where(turned, jnp.sin(angle), 0.0)
-        sine = jnp.where(lane < HEAD_DIM // 2, -sine, sine)
-        turned = total * cosine + pltpu.roll(total, HEAD_DIM // 2, 1) * sine
+        turned = total * cos_buf[...] + pltpu.roll(total, HEAD_DIM // 2, 1) * sin_buf[...]
         qkv[...] = turned.astype(BF16)
         query_all[my_b] = turned[0 : query_all.shape[1]].astype(BF16)
 
@@ -232,8 +231,7 @@
             if per > 1:
                 dst = lax.rem(me + off, n_seq)
             else:
-                other = jnp.where(off <= lines, 1 - side, side)
-                dst = 2 * lax.rem(line + n_seq - off, lines) + other
+                dst = 2 * lax.rem(line + n_seq - off // 2, lines) + lax.rem(side + off, 2)
             copy_gather(query_all, s2_sem, r2_sem, my_b, dst).start()
 
     on_owner(owner_rotate)
@@ -256,9 +254,9 @@
         return [
             pltpu.make_async_remote_copy(
                 src_ref=source.at[b],
-                dst_ref=target.at[src // 2],
+                dst_ref=target.at[src],
                 send_sem=send_sem.at[b],
-                recv_sem=recv_sem.at[src // 2],
+                recv_sem=recv_sem.at[src],
                 device_id=(b * per, hd),
                 device_id_type=MESH,
             )
@@ -268,32 +266,7 @@
             )
         ]
 
-    def copies_across(b):
-        return [
-            pltpu.make_async_remote_copy(
-                src_ref=source.at[b],
-                dst_ref=target.at[b],
-                send_sem=send_sem.at[b],
-                recv_sem=recv_sem.at[b],
-                device_id=(partner, hd),
-                device_id_type=MESH,
-            )
-            for source, target, send_sem, recv_sem in (
-                (sendml, pairml, sm_sem, pm_sem),
-                (send3, pair3, s3_sem, p3_sem),
-            )
-        ]
-
-    @pl.loop(0, batch)
-    def _(i):
-        b = use_order(i)
-
-        @pl.when(b * per != me)
-        def _():
-            copy_gather(query_all, s2_sem, r2_sem, b, me).wait_recv()
-
-        for copy in cache_copies(b):
-            copy.wait()
+    def attend(b):
         query = query_all[b].astype(F32)[0:qrows]
         row = lax.broadcasted_iota(jnp.int32, query.shape, 0)
         spread = jnp.concatenate(
@@ -328,36 +301,33 @@
             for kv in range(kv_local):
                 r0 = half * qrows + kv * grows
                 blocks.append(values[r0 : r0 + grows, kv * HEAD_DIM : (kv + 1) * HEAD_DIM])
-        values = jnp.concatenate(blocks, axis=0)
-        peak = jnp.concatenate([t_peak, d_peak], axis=0)
-        total = jnp.concatenate([t_total, d_total], axis=0)
-
-        @pl.when(is_own(b))
-        def _():
-            recv3[line] = values.astype(BF16)
-            recvml[line] = statistics(peak, total)
-
-        @pl.when(jnp.logical_not(is_mine(b)))
-        def _():
-            send3[b] = values.astype(BF16)
-            sendml[b] = statistics(peak, total)
-            for copy in copies_across(b):
-                copy.start()
-
-        @pl.when(is_mine(b) & jnp.logical_not(is_own(b)))
-        def _():
-            for copy in copies_across(b):
-                copy.wait_recv()
-            pairs[0:2, :] = pairml[b]
-            theirs = pairs[...].T
-            their_peak = theirs[0:srows, 0:1]
-            joint = jnp.maximum(peak, their_peak)
-            ours = jnp.exp2(peak - joint)
-            other = jnp.exp2(their_peak - joint)
-            send3[b] = (values * ours + pair3[b].astype(F32) * other).astype(BF16)
-            sendml[b] = statistics(joint, total * ours + theirs[0:srows, 1:2] * other)
-            for copy in copies_up(b, me):
-                copy.start()
+        send3[b] = jnp.concatenate(blocks, axis=0).astype(BF16)
+        sendml[b] = statistics(
+            jnp.concatenate([t_peak, d_peak], axis=0),
+            jnp.concatenate([t_total, d_total], axis=0),
+        )
+
+    together = 2
+
+    @pl.loop(0, batch // together)
+    def _(i):
+        several = [use_order(i * together + at) for at in range(together)]
+        for b in several:
+
+            @pl.when(jnp.logical_not(is_own(b)))
+            def _(b=b):
+                copy_gather(query_all, s2_sem, r2_sem, b, me).wait_recv()
+
+            for copy in cache_copies(b):
+                copy.wait()
+        for b in several:
+            attend(b)
+        for b in several:
+
+            @pl.when(jnp.logical_not(is_own(b)))
+            def _(b=b):
+                for copy in copies_up(b, me):
+                    copy.start()
 
     def owner_merge():
         rows_all = qkv[...].astype(F32)
@@ -380,22 +350,19 @@
         moved = pltpu.roll(rows_all, rows_all.shape[0] - shift, 0)
         moved = jnp.where((vrow >= 0) & (vrow < shift), moved, 0.0).astype(BF16)
         values = jnp.dot(weights, moved, preferred_element_type=F32)
-        fresh = lines + 1
-        recv3[fresh] = jnp.concatenate([values, values], axis=0).astype(BF16)
-        recvml[fresh] = statistics(
+        recv3[n_seq] = jnp.concatenate([values, values], axis=0).astype(BF16)
+        recvml[n_seq] = statistics(
             jnp.concatenate([peak, peak], axis=0), jnp.concatenate([total, total], axis=0)
         )
-        for copy in copies_across(my_b):
-            copy.wait_recv()
-        recv3[lines] = pair3[my_b]
-        recvml[lines] = pairml[my_b]
-
-        @pl.loop(1, lines)
+        recv3[me] = send3[my_b]
+        recvml[me] = sendml[my_b]
+
+        @pl.loop(1, n_seq)
         def _(off):
-            for copy in copies_up(my_b, 2 * lax.rem(line + off, lines)):
+            for copy in copies_up(my_b, lax.rem(me + off, n_seq)):
                 copy.wait_recv()
 
-        n_src = lines + 2
+        n_src = n_seq + 1
         for s in range(n_src):
             both = recvml[s]
             mscr[s : s + 1, :] = both[0:1]
@@ -598,7 +565,7 @@
     part_rows = round_up(-(-n_rows // row_parts), 16)
     part_cols = out_cols // col_parts
     all_rows = part_rows * row_parts
-    n_src = n_seq // 2 + 2
+    n_src = n_seq + 1
     src_rows = round_up(n_src, 8)
     qpad = round_up(verify * heads, 16)
     dims = (n_seq, n_head, batch, verify, kv_local, heads, ctx_local, col_parts)
@@ -613,8 +580,8 @@
     target, drafted = pl.pallas_call(
         functools.partial(kernel, dims),
         out_shape=(
-            jax.ShapeDtypeStruct((batch * verify, out_cols), BF16),
-            jax.ShapeDtypeStruct((batch, draft, out_cols), BF16),
+            pltpu.VMEM((batch * verify, out_cols), BF16),
+            pltpu.VMEM((batch, draft, out_cols), BF16),
         ),
         in_specs=[vmem, vmem, smem, smem] + [hbm] * 6,
         out_specs=(vmem, vmem),
@@ -630,11 +597,10 @@
             pltpu.VMEM((batch, qpad, HEAD_DIM), BF16),
             pltpu.VMEM((batch, srows, HEAD_DIM), BF16),
             pltpu.VMEM((n_src, srows, HEAD_DIM), BF16),
-            pltpu.VMEM((batch, srows, HEAD_DIM), BF16),
             pltpu.VMEM((batch, 2, lanes), F32),
             pltpu.VMEM((n_src, 2, lanes), F32),
-            pltpu.VMEM((batch, 2, lanes), F32),
-            pltpu.VMEM((HEAD_DIM, lanes), F32),
+            pltpu.VMEM((rows1, HEAD_DIM), F32),
+            pltpu.VMEM((rows1, HEAD_DIM), F32),
             pltpu.VMEM((src_rows, lanes), F32),
             pltpu.VMEM((src_rows, lanes), F32),
             pltpu.VMEM((HEAD_DIM, lanes), F32),
@@ -655,11 +621,9 @@
             dma((n_seq,)),
             dma((batch,)),
             dma((batch,)),
-            dma((n_seq // 2,)),
-            dma((batch,)),
-            dma((batch,)),
-            dma((n_seq // 2,)),
-            dma((batch,)),
+            dma((n_seq,)),
+            dma((batch,)),
+            dma((n_seq,)),
             dma((n_seq,)),
             dma((batch,)),
             dma((batch,)),

time: 50.4 us -> 48.4 us (0.960)
  local copies, waits for them, and re-layouts: 3.02 us -> 1.27 us
    unnamed x2, local copies, waits for them, and re-layouts: 3.02 us -> 1.27 us
where the time goes in v3:
time: 48.4 us; the launch traced here: 48.2 us
  Pallas kernels  46.3 us (96%)
  local copies, waits for them, and re-layouts  1.27 us (3%)
  between operations  0.64 us (1%)
    pallas_call x1, Pallas kernels, per_device(): pl.pallas_call(functools.partial(kernel, dims), out_shape=(pltpu.VMEM((ba...  46.3 us
    unnamed x2, local copies, waits for them, and re-layouts  1.27 us

profile of v3, /device:TPU:0, one launch (start us, length us, event | category | flops | bytes accessed | tf_op | source)
XLA Modules:
  0.0 48.2 jit_solution(5855039636858587269)
XLA Ops:
  0.6 46.3 %verify_round.1 = (bf16[40,1024]{1,0:T(8,128)(2,1)S(1)}, bf16[8,4,1024]{2,1,0:T(4,128)(2,1)S(1)}) custom-call(bf16[40,1024]{1,0:T(8,128)(2,1)} %bitcast.7, f32[1,128]{1,0:T(1,128)} %constant.2.clone.inv, s32[8]{0:T(128)} %ctx.1, s32[8,8]{1,0:T(8,128)} %keep.1, bf16[1024,2048]{1,0:T(8,128)(2,1)} %wq.1, bf16[1024,256]{1,0:T(8,128)(2,1)} %wk.1, ...), custom_call_target="tpu_custom_call" | custom-call | tf_op jit(solution)/shard_map/verify_round/pallas_call | solution.py:580
  46.9 0.6 %copy.14 = bf16[8,5,1024]{2,0,1:T(8,128)(2,1)} copy(bf16[8,5,1024]{2,0,1:T(8,128)(2,1)S(1)} %bitcast.6) | data formatting | bytes 163840
  47.5 0.6 %copy.15 = bf16[8,4,1024]{2,1,0:T(4,128)(2,1)} copy(bf16[8,4,1024]{2,1,0:T(4,128)(2,1)S(1)} %get-tuple-element.7) | data formatting | bytes 131072

commit v4 on v3

--- a/solution.py
+++ b/solution.py
@@ -23,10 +23,10 @@
 
 def kernel(
     dims,
-    hid,
-    inv,
-    ctx,
-    keep,
+    hid_in,
+    inv_in,
+    ctx_in,
+    keep_in,
     wq,
     wk,
     wv,
@@ -35,6 +35,11 @@
     vc,
     out_v,
     out_d,
+    hid,
+    inv,
+    ctx,
+    keep,
+    small_sem,
     w_buf,
     wo_buf,
     k_buf,
@@ -55,6 +60,8 @@
     coefs,
     coef_t,
     att,
+    spare,
+    dense,
     att32,
     x_buf,
     send4,
@@ -96,6 +103,7 @@
     my_b = me // per
     scale = HEAD_DIM ** (-0.5) * math.log2(math.e)
     rows1 = send1.shape[1]
+    crows = att.shape[1]
     lines = n_seq // 2
     line, side = me // 2, lax.rem(me, 2)
     partner = me + 1 - 2 * side
@@ -131,6 +139,15 @@
         pl.semaphore_signal(
             barrier, inc=1, device_id=(me, lax.rem(hd + off, n_head)), device_id_type=MESH
         )
+
+    small = [
+        pltpu.make_async_copy(src, dst, small_sem.at[at])
+        for at, (src, dst) in enumerate(
+            ((ctx_in, ctx), (inv_in, inv), (hid_in, hid), (keep_in, keep))
+        )
+    ]
+    for copy in small:
+        copy.start()
 
     step = min(512, q_cols)
     pieces = [(wq, c, step, c) for c in range(0, q_cols, step)]
@@ -150,23 +167,58 @@
         )
 
     def rotation():
-        shape = cos_buf.shape
-        row = lax.broadcasted_iota(jnp.int32, shape, 0)
+        shape = (8, HEAD_DIM)
         lane = lax.broadcasted_iota(jnp.int32, shape, 1)
-        slot = lax.div(row, verify)
-        pos = (ctx[my_b] + (row - slot * verify)).astype(F32)
+        pos = (ctx[my_b] + lax.broadcasted_iota(jnp.int32, shape, 0)).astype(F32)
         angle = pos * inv[...]
-        turned = slot < heads + kv_local
-        sine = jnp.where(turned, jnp.sin(angle), 0.0)
-        cos_buf[...] = jnp.where(turned, jnp.cos(angle), 1.0)
-        sin_buf[...] = jnp.where(lane < HEAD_DIM // 2, -sine, sine)
-
+        cosine = jnp.cos(angle)
+        sine = jnp.sin(angle)
+        sine = jnp.where(lane < HEAD_DIM // 2, -sine, sine)
+        cos_buf[...] = jnp.ones_like(cos_buf)
+        sin_buf[...] = jnp.zeros_like(sin_buf)
+        for slot in range(heads + kv_local):
+            r0 = slot * verify
+            cos_buf[r0 : r0 + 8, :] = cosine
+            sin_buf[r0 : r0 + 8, :] = sine
+        r0 = (heads + kv_local) * verify
+        cos_buf[r0 : r0 + 8, :] = jnp.ones(shape, F32)
+        sin_buf[r0 : r0 + 8, :] = jnp.zeros(shape, F32)
+
+    for copy in small:
+        copy.wait()
     on_owner(rotation)
 
     pack[...] = jnp.zeros_like(pack)
     coefs[...] = jnp.zeros_like(coefs)
     x_in = hid[...]
-    for copy, (src, c0, width, d0) in zip(w_copies, pieces):
+    def copy1(part, b, src):
+        rows = pl.ds(*parts[part])
+        return pltpu.make_async_remote_copy(
+            src_ref=send1.at[b, rows],
+            dst_ref=recv1.at[src, rows],
+            send_sem=s1_sem.at[part, b],
+            recv_sem=r1_sem.at[part, src],
+            device_id=(b * per, hd),
+            device_id_type=MESH,
+        )
+
+    def send_part(part):
+        r0, count = parts[part]
+
+        @pl.loop(0, batch)
+        def _(i):
+            b = lax.rem(my_b + 1 + i, batch)
+            rows = pl.ds(pl.multiple_of(b * rows1 + r0, 16), count)
+            send1[b, r0 : r0 + count, :] = pack[rows, :].astype(BF16)
+
+            @pl.when(b * per != me)
+            def _():
+                copy1(part, b, me).start()
+
+    early = rows1 // 2 // 16 * 16
+    parts = ((0, early), (early, rows1 - early))
+    sent_early = False
+    for at, (copy, (src, c0, width, d0)) in enumerate(zip(w_copies, pieces)):
         copy.wait()
         piece = jnp.dot(x_in, w_buf[:, d0 : d0 + width], preferred_element_type=F32)
         for s in range(width // HEAD_DIM):
@@ -175,6 +227,11 @@
                 pack[pl.ds(slot * verify + j, batch, stride=rows1), :] = piece[
                     j * batch : (j + 1) * batch, s * HEAD_DIM : (s + 1) * HEAD_DIM
                 ]
+        if not sent_early and (d0 + width) // HEAD_DIM * verify >= early:
+            sent_early = True
+            pl.semaphore_wait(barrier, n_seq - 1 + n_head - 1)
+            send_part(0)
+    send_part(1)
 
     @pl.loop(0, batch)
     def _(i):
@@ -183,27 +240,6 @@
 
     wo_copy = pltpu.make_async_copy(wo, wo_buf, wo_sem)
     wo_copy.start()
-
-    pl.semaphore_wait(barrier, n_seq - 1 + n_head - 1)
-
-    def copy1(b, src):
-        return pltpu.make_async_remote_copy(
-            src_ref=send1.at[b],
-            dst_ref=recv1.at[src],
-            send_sem=s1_sem.at[b],
-            recv_sem=r1_sem.at[src],
-            device_id=(b * per, hd),
-            device_id_type=MESH,
-        )
-
-    @pl.loop(0, batch)
-    def _(i):
-        b = lax.rem(my_b + 1 + i, batch)
-        send1[b] = pack[pl.ds(pl.multiple_of(b * rows1, 16), rows1), :].astype(BF16)
-
-        @pl.when(b * per != me)
-        def _():
-            copy1(b, me).start()
 
     def copy_gather(buf, send_sem, recv_sem, b, dst):
         return pltpu.make_async_remote_copy(
@@ -218,7 +254,8 @@
     def owner_rotate():
         def add(off, acc):
             src = lax.rem(me + off, n_seq)
-            copy1(my_b, src).wait_recv()
+            for part in range(2):
+                copy1(part, my_b, src).wait_recv()
             return acc + recv1[src].astype(F32)
 
         total = lax.fori_loop(1, n_seq, add, send1[my_b].astype(F32))
@@ -377,7 +414,14 @@
         acc = jnp.zeros((srows, HEAD_DIM), F32)
         for s in range(n_src):
             acc = acc + coef_t[0:srows, s : s + 1] * recv3[s].astype(F32)
-        att[my_b] = acc.astype(BF16)
+        spare[0:srows, :] = acc
+        spare[srows : srows + 8, :] = jnp.zeros((8, HEAD_DIM), F32)
+        dense[...] = jnp.zeros_like(dense)
+        dense[0:qrows, :] = acc[0:qrows]
+        for h in range(heads):
+            r0, r1 = qrows + h * draft, qrows + h * verify
+            dense[r0 : r0 + 8, :] = spare[r1 : r1 + 8, :]
+        att[my_b] = dense[0:crows, :].astype(BF16)
 
         copy_gather(att, s5_sem, r5_sem, my_b, partner).start()
 
@@ -410,17 +454,17 @@
         def _():
             copy_forward(b).start()
 
-        att32[pl.ds(pl.multiple_of(b * srows, 8), srows), :] = att[b].astype(F32)
-
-    planes = [j for j in range(verify)] + [qrows + j for j in range(draft)]
+        att32[pl.ds(pl.multiple_of(b * crows, 16), crows), :] = att[b].astype(F32)
+
+    planes = [(j, verify) for j in range(verify)]
+    planes += [(qrows + j, draft) for j in range(draft)]
     for pair in range(x_buf.shape[0] // 16):
         for h in range(heads):
             halves = []
             for at in (2 * pair, 2 * pair + 1):
                 if at < len(planes):
-                    halves.append(
-                        att32[pl.ds(planes[at] + h * verify, batch, stride=srows), :]
-                    )
+                    start, jump = planes[at]
+                    halves.append(att32[pl.ds(start + h * jump, batch, stride=crows), :])
                 else:
                     halves.append(jnp.zeros((batch, HEAD_DIM), F32))
             x_buf[16 * pair : 16 * pair + 16, h * HEAD_DIM : (h + 1) * HEAD_DIM] = (
@@ -507,7 +551,8 @@
     def _(b):
         @pl.when(b * per != me)
         def _():
-            copy1(b, me).wait_send()
+            for part in range(2):
+                copy1(part, b, me).wait_send()
             for copy in copies_up(b, me):
                 copy.wait_send()
 
@@ -558,6 +603,7 @@
     slots = heads + 2 * kv_local
     rows1 = round_up(verify * slots, 16)
     srows = 2 * verify * heads
+    crows = round_up((verify + draft) * heads, 16)
     lanes = round_up(srows, HEAD_DIM)
     n_rows = batch * (verify + draft)
     col_parts = math.gcd(n_head, out_cols // HEAD_DIM)
@@ -574,7 +620,6 @@
     inverse = jnp.asarray(np.concatenate([inverse, inverse])[None, :])
 
     vmem = pl.BlockSpec(memory_space=pltpu.VMEM)
-    smem = pl.BlockSpec(memory_space=pltpu.SMEM)
     hbm = pl.BlockSpec(memory_space=pl.ANY)
     dma = pltpu.SemaphoreType.DMA
     target, drafted = pl.pallas_call(
@@ -583,9 +628,14 @@
             pltpu.VMEM((batch * verify, out_cols), BF16),
             pltpu.VMEM((batch, draft, out_cols), BF16),
         ),
-        in_specs=[vmem, vmem, smem, smem] + [hbm] * 6,
+        in_specs=[hbm] * 10,
         out_specs=(vmem, vmem),
         scratch_shapes=[
+            pltpu.VMEM((verify * batch, width), BF16),
+            pltpu.VMEM(inverse.shape, F32),
+            pltpu.SMEM(context_lengths.shape, jnp.int32),
+            pltpu.SMEM(keep_blocks.shape, jnp.int32),
+            dma((4,)),
             pltpu.VMEM((width, q_cols + 2 * kv_cols), BF16),
             pltpu.VMEM(w_out.shape, BF16),
             pltpu.VMEM(key_cache.shape, BF16),
@@ -605,8 +655,10 @@
             pltpu.VMEM((src_rows, lanes), F32),
             pltpu.VMEM((HEAD_DIM, lanes), F32),
             pltpu.VMEM((lanes, HEAD_DIM), F32),
-            pltpu.VMEM((batch, srows, HEAD_DIM), BF16),
-            pltpu.VMEM((batch * srows, HEAD_DIM), F32),
+            pltpu.VMEM((batch, crows, HEAD_DIM), BF16),
+            pltpu.VMEM((srows + 8, HEAD_DIM), F32),
+            pltpu.VMEM((crows + 8, HEAD_DIM), F32),
+            pltpu.VMEM((batch * crows, HEAD_DIM), F32),
             pltpu.VMEM((all_rows, q_cols), BF16),
             pltpu.VMEM((n_head, part_rows, part_cols), BF16),
             pltpu.VMEM((n_head, part_rows, part_cols), BF16),
@@ -616,8 +668,8 @@
             dma,
             dma((batch,)),
             dma((batch,)),
-            dma((batch,)),
-            dma((n_seq,)),
+            dma((2, batch)),
+            dma((2, n_seq)),
             dma((n_seq,)),
             dma((batch,)),
             dma((batch,)),

time: 48.4 us -> 46.7 us (0.965)
  Pallas kernels: 46.3 us -> 44.7 us
    pallas_call x1, Pallas kernels: 46.3 us -> 44.7 us  [per_device(): pl.pallas_call(functools.partial(kernel, dims), out_shape=(pltpu.VMEM((ba...]
where the time goes in v4:
time: 46.7 us; the launch traced here: 46.6 us
  Pallas kernels  44.7 us (96%)
  local copies, waits for them, and re-layouts  1.27 us (3%)
  between operations  0.64 us (1%)
    pallas_call x1, Pallas kernels, per_device(): pl.pallas_call(functools.partial(kernel, dims), out_shape=(pltpu.VMEM((ba...  44.7 us
    unnamed x2, local copies, waits for them, and re-layouts  1.27 us

profile of v4, /device:TPU:0, one launch (start us, length us, event | category | flops | bytes accessed | tf_op | source)
XLA Modules:
  0.0 46.6 jit_solution(98295146073457737)
XLA Ops:
  0.6 44.7 %verify_round.1 = (bf16[40,1024]{1,0:T(8,128)(2,1)S(1)}, bf16[8,4,1024]{2,1,0:T(4,128)(2,1)S(1)}) custom-call(bf16[40,1024]{1,0:T(8,128)(2,1)} %bitcast.7, f32[1,128]{1,0:T(1,128)} %constant.2.clone.inv_in, s32[8]{0:T(128)} %ctx_in.1, s32[8,8]{1,0:T(8,128)} %keep_in.1, bf16[1024,2048]{1,0:T(8,128)(2,1)} %wq.1, bf16[1024,256]{1,0:T(8,128)(2,1)} %wk.1, ...), custom_call_target="tpu_custom_call" | custom-call | tf_op jit(solution)/shard_map/verify_round/pallas_call | solution.py:625
  45.3 0.6 %copy.14 = bf16[8,5,1024]{2,0,1:T(8,128)(2,1)} copy(bf16[8,5,1024]{2,0,1:T(8,128)(2,1)S(1)} %bitcast.6) | data formatting | bytes 163840
  45.9 0.6 %copy.15 = bf16[8,4,1024]{2,1,0:T(4,128)(2,1)} copy(bf16[8,4,1024]{2,1,0:T(4,128)(2,1)S(1)} %get-tuple-element.7) | data formatting | bytes 131072

commit v5 on v4

--- a/solution.py
+++ b/solution.py
@@ -47,6 +47,7 @@
     pack,
     send1,
     recv1,
+    pair1,
     qkv,
     query_all,
     send3,
@@ -74,6 +75,7 @@
     v_sem,
     s1_sem,
     r1_sem,
+    p1_sem,
     s2_sem,
     r2_sem,
     s3_sem,
@@ -118,6 +120,21 @@
             return lax.rem(my_b + i, batch)
         return 2 * lax.rem(line + i, lines) + jnp.where(i < lines, side, 1 - side)
 
+    def side_loop(mine, body):
+        if per > 1:
+
+            @pl.loop(0, batch)
+            def _(i):
+                b = lax.rem(my_b + i, batch)
+                pl.when(is_mine(b) if mine else jnp.logical_not(is_mine(b)))(
+                    functools.partial(body, b)
+                )
+        else:
+
+            @pl.loop(0, lines)
+            def _(i):
+                body(2 * lax.rem(line + 1 + i, lines) + (side if mine else 1 - side))
+
     def is_mine(b):
         return lax.rem(b * per, 2) == side
 
@@ -190,30 +207,52 @@
 
     pack[...] = jnp.zeros_like(pack)
     coefs[...] = jnp.zeros_like(coefs)
+    spare[...] = jnp.zeros_like(spare)
+    dense[...] = jnp.zeros_like(dense)
     x_in = hid[...]
-    def copy1(part, b, src):
+    def copy_pair(part, b):
         rows = pl.ds(*parts[part])
         return pltpu.make_async_remote_copy(
             src_ref=send1.at[b, rows],
-            dst_ref=recv1.at[src, rows],
+            dst_ref=pair1.at[b, rows],
             send_sem=s1_sem.at[part, b],
-            recv_sem=r1_sem.at[part, src],
+            recv_sem=p1_sem.at[part, b],
+            device_id=(partner, hd),
+            device_id_type=MESH,
+        )
+
+    def copy1(b, src_line):
+        return pltpu.make_async_remote_copy(
+            src_ref=send1.at[b],
+            dst_ref=recv1.at[src_line],
+            send_sem=s1_sem.at[0, b],
+            recv_sem=r1_sem.at[src_line],
             device_id=(b * per, hd),
             device_id_type=MESH,
         )
 
+    def pack_rows(b, r0, count):
+        return pack[pl.ds(pl.multiple_of(b * rows1 + r0, 16), count), :]
+
     def send_part(part):
         r0, count = parts[part]
 
-        @pl.loop(0, batch)
-        def _(i):
-            b = lax.rem(my_b + 1 + i, batch)
-            rows = pl.ds(pl.multiple_of(b * rows1 + r0, 16), count)
-            send1[b, r0 : r0 + count, :] = pack[rows, :].astype(BF16)
-
-            @pl.when(b * per != me)
-            def _():
-                copy1(part, b, me).start()
+        def body(b):
+            send1[b, r0 : r0 + count, :] = pack_rows(b, r0, count).astype(BF16)
+            copy_pair(part, b).start()
+
+        side_loop(False, body)
+
+    def paired_sum(b):
+        for part in range(2):
+            copy_pair(part, b).wait_recv()
+        return pack_rows(b, 0, rows1) + pair1[b].astype(F32)
+
+    def send_line(b):
+        @pl.when(jnp.logical_not(is_own(b)))
+        def _():
+            send1[b] = paired_sum(b).astype(BF16)
+            copy1(b, line).start()
 
     early = rows1 // 2 // 16 * 16
     parts = ((0, early), (early, rows1 - early))
@@ -232,6 +271,7 @@
             pl.semaphore_wait(barrier, n_seq - 1 + n_head - 1)
             send_part(0)
     send_part(1)
+    side_loop(True, send_line)
 
     @pl.loop(0, batch)
     def _(i):
@@ -253,12 +293,11 @@
 
     def owner_rotate():
         def add(off, acc):
-            src = lax.rem(me + off, n_seq)
-            for part in range(2):
-                copy1(part, my_b, src).wait_recv()
+            src = lax.rem(line + off, lines)
+            copy1(my_b, src).wait_recv()
             return acc + recv1[src].astype(F32)
 
-        total = lax.fori_loop(1, n_seq, add, send1[my_b].astype(F32))
+        total = lax.fori_loop(1, lines, add, paired_sum(my_b))
         turned = total * cos_buf[...] + pltpu.roll(total, HEAD_DIM // 2, 1) * sin_buf[...]
         qkv[...] = turned.astype(BF16)
         query_all[my_b] = turned[0 : query_all.shape[1]].astype(BF16)
@@ -272,6 +311,15 @@
             copy_gather(query_all, s2_sem, r2_sem, my_b, dst).start()
 
     on_owner(owner_rotate)
+
+    def compact(value, at):
+        loose = spare.at[at]
+        loose[0:srows, :] = value
+        tight = dense.at[at]
+        for h in range(heads):
+            r0, r1 = qrows + h * draft, qrows + h * verify
+            tight[r0 : r0 + 8, :] = loose[r1 : r1 + 8, :]
+        return jnp.concatenate([value[0:qrows], tight[qrows:crows, :]], axis=0)
 
     def statistics(peak, total):
         lane = lax.broadcasted_iota(jnp.int32, (srows, HEAD_DIM), 1)
@@ -303,7 +351,7 @@
             )
         ]
 
-    def attend(b):
+    def attend(b, at):
         query = query_all[b].astype(F32)[0:qrows]
         row = lax.broadcasted_iota(jnp.int32, query.shape, 0)
         spread = jnp.concatenate(
@@ -338,7 +386,7 @@
             for kv in range(kv_local):
                 r0 = half * qrows + kv * grows
                 blocks.append(values[r0 : r0 + grows, kv * HEAD_DIM : (kv + 1) * HEAD_DIM])
-        send3[b] = jnp.concatenate(blocks, axis=0).astype(BF16)
+        send3[b] = compact(jnp.concatenate(blocks, axis=0), at).astype(BF16)
         sendml[b] = statistics(
             jnp.concatenate([t_peak, d_peak], axis=0),
             jnp.concatenate([t_total, d_total], axis=0),
@@ -357,8 +405,8 @@
 
             for copy in cache_copies(b):
                 copy.wait()
-        for b in several:
-            attend(b)
+        for at, b in enumerate(several):
+            attend(b, at)
         for b in several:
 
             @pl.when(jnp.logical_not(is_own(b)))
@@ -387,7 +435,7 @@
         moved = pltpu.roll(rows_all, rows_all.shape[0] - shift, 0)
         moved = jnp.where((vrow >= 0) & (vrow < shift), moved, 0.0).astype(BF16)
         values = jnp.dot(weights, moved, preferred_element_type=F32)
-        recv3[n_seq] = jnp.concatenate([values, values], axis=0).astype(BF16)
+        recv3[n_seq] = compact(jnp.concatenate([values, values], axis=0), 0).astype(BF16)
         recvml[n_seq] = statistics(
             jnp.concatenate([peak, peak], axis=0), jnp.concatenate([total, total], axis=0)
         )
@@ -410,19 +458,11 @@
         norm = jnp.sum(factor * l_all, axis=0, keepdims=True)
         norm = jnp.where(norm > 0.0, norm, 1.0)
         coefs[0:n_src, :] = factor / norm
-        coef_t[...] = coefs[...].T
-        acc = jnp.zeros((srows, HEAD_DIM), F32)
+        coef_t[0:crows, :] = compact(coefs[...].T[0:srows], 0)
+        acc = jnp.zeros((crows, HEAD_DIM), F32)
         for s in range(n_src):
-            acc = acc + coef_t[0:srows, s : s + 1] * recv3[s].astype(F32)
-        spare[0:srows, :] = acc
-        spare[srows : srows + 8, :] = jnp.zeros((8, HEAD_DIM), F32)
-        dense[...] = jnp.zeros_like(dense)
-        dense[0:qrows, :] = acc[0:qrows]
-        for h in range(heads):
-            r0, r1 = qrows + h * draft, qrows + h * verify
-            dense[r0 : r0 + 8, :] = spare[r1 : r1 + 8, :]
-        att[my_b] = dense[0:crows, :].astype(BF16)
-
+            acc = acc + coef_t[0:crows, s : s + 1] * recv3[s].astype(F32)
+        att[my_b] = acc.astype(BF16)
         copy_gather(att, s5_sem, r5_sem, my_b, partner).start()
 
         @pl.loop(1, lines)
@@ -547,12 +587,22 @@
             axis=1,
         ).astype(BF16)
 
+    def pair_sent(b):
+        for part in range(2):
+            copy_pair(part, b).wait_send()
+
+    def line_sent(b):
+        @pl.when(jnp.logical_not(is_own(b)))
+        def _():
+            copy1(b, line).wait_send()
+
+    side_loop(False, pair_sent)
+    side_loop(True, line_sent)
+
     @pl.loop(0, batch)
     def _(b):
         @pl.when(b * per != me)
         def _():
-            for part in range(2):
-                copy1(part, b, me).wait_send()
             for copy in copies_up(b, me):
                 copy.wait_send()
 
@@ -642,11 +692,12 @@
             pltpu.VMEM(value_cache.shape, BF16),
             pltpu.VMEM((batch * rows1, HEAD_DIM), F32),
             pltpu.VMEM((batch, rows1, HEAD_DIM), BF16),
-            pltpu.VMEM((n_seq, rows1, HEAD_DIM), BF16),
+            pltpu.VMEM((n_seq // 2, rows1, HEAD_DIM), BF16),
+            pltpu.VMEM((batch, rows1, HEAD_DIM), BF16),
             pltpu.VMEM((rows1, HEAD_DIM), BF16),
             pltpu.VMEM((batch, qpad, HEAD_DIM), BF16),
-            pltpu.VMEM((batch, srows, HEAD_DIM), BF16),
-            pltpu.VMEM((n_src, srows, HEAD_DIM), BF16),
+            pltpu.VMEM((batch, crows, HEAD_DIM), BF16),
+            pltpu.VMEM((n_src, crows, HEAD_DIM), BF16),
             pltpu.VMEM((batch, 2, lanes), F32),
             pltpu.VMEM((n_src, 2, lanes), F32),
             pltpu.VMEM((rows1, HEAD_DIM), F32),
@@ -656,8 +707,8 @@
             pltpu.VMEM((HEAD_DIM, lanes), F32),
             pltpu.VMEM((lanes, HEAD_DIM), F32),
             pltpu.VMEM((batch, crows, HEAD_DIM), BF16),
-            pltpu.VMEM((srows + 8, HEAD_DIM), F32),
-            pltpu.VMEM((crows + 8, HEAD_DIM), F32),
+            pltpu.VMEM((2, srows + 8, HEAD_DIM), F32),
+            pltpu.VMEM((2, crows + 8, HEAD_DIM), F32),
             pltpu.VMEM((batch * crows, HEAD_DIM), F32),
             pltpu.VMEM((all_rows, q_cols), BF16),
             pltpu.VMEM((n_head, part_rows, part_cols), BF16),
@@ -669,7 +720,8 @@
             dma((batch,)),
             dma((batch,)),
             dma((2, batch)),
-            dma((2, n_seq)),
+            dma((n_seq // 2,)),
+            dma((2, batch)),
             dma((n_seq,)),
             dma((batch,)),
             dma((batch,)),

time: 46.7 us -> 47 us (level)
  no operation moved by 1% of the time
where the time goes in v5:
time: 47 us; the launch traced here: 46.8 us
  Pallas kernels  44.9 us (96%)
  local copies, waits for them, and re-layouts  1.27 us (3%)
  between operations  0.64 us (1%)
    pallas_call x1, Pallas kernels, per_device(): pl.pallas_call(functools.partial(kernel, dims), out_shape=(pltpu.VMEM((ba...  44.9 us
    unnamed x2, local copies, waits for them, and re-layouts  1.27 us

profile of v5, /device:TPU:0, one launch (start us, length us, event | category | flops | bytes accessed | tf_op | source)
XLA Modules:
  0.0 46.8 jit_solution(2948823743311267598)
XLA Ops:
  0.6 44.9 %verify_round.1 = (bf16[40,1024]{1,0:T(8,128)(2,1)S(1)}, bf16[8,4,1024]{2,1,0:T(4,128)(2,1)S(1)}) custom-call(bf16[40,1024]{1,0:T(8,128)(2,1)} %bitcast.7, f32[1,128]{1,0:T(1,128)} %constant.2.clone.inv_in, s32[8]{0:T(128)} %ctx_in.1, s32[8,8]{1,0:T(8,128)} %keep_in.1, bf16[1024,2048]{1,0:T(8,128)(2,1)} %wq.1, bf16[1024,256]{1,0:T(8,128)(2,1)} %wk.1, ...), custom_call_target="tpu_custom_call" | custom-call | tf_op jit(solution)/shard_map/verify_round/pallas_call | solution.py:675
  45.6 0.6 %copy.14 = bf16[8,5,1024]{2,0,1:T(8,128)(2,1)} copy(bf16[8,5,1024]{2,0,1:T(8,128)(2,1)S(1)} %bitcast.6) | data formatting | bytes 163840
  46.2 0.6 %copy.15 = bf16[8,4,1024]{2,1,0:T(4,128)(2,1)} copy(bf16[8,4,1024]{2,1,0:T(4,128)(2,1)S(1)} %get-tuple-element.7) | data formatting | bytes 131072

commit v6 on v4

--- a/solution.py
+++ b/solution.py
@@ -82,7 +82,6 @@
     rm_sem,
     s5_sem,
     r5_sem,
-    f5_sem,
     s4_sem,
     r4_sem,
     s6_sem,
@@ -106,20 +105,11 @@
     crows = att.shape[1]
     lines = n_seq // 2
     line, side = me // 2, lax.rem(me, 2)
-    partner = me + 1 - 2 * side
 
     def use_order(i):
         if per > 1:
             return lax.rem(my_b + i, batch)
         return 2 * lax.rem(line + i // 2, lines) + lax.rem(side + i, 2)
-
-    def gather_order(i):
-        if per > 1:
-            return lax.rem(my_b + i, batch)
-        return 2 * lax.rem(line + i, lines) + jnp.where(i < lines, side, 1 - side)
-
-    def is_mine(b):
-        return lax.rem(b * per, 2) == side
 
     def is_own(b):
         return b * per == me
@@ -190,6 +180,8 @@
 
     pack[...] = jnp.zeros_like(pack)
     coefs[...] = jnp.zeros_like(coefs)
+    spare[...] = jnp.zeros_like(spare)
+    dense[...] = jnp.zeros_like(dense)
     x_in = hid[...]
     def copy1(part, b, src):
         rows = pl.ds(*parts[part])
@@ -273,6 +265,15 @@
 
     on_owner(owner_rotate)
 
+    def compact(value, at):
+        loose = spare.at[at]
+        loose[0:srows, :] = value
+        tight = dense.at[at]
+        for h in range(heads):
+            r0, r1 = qrows + h * draft, qrows + h * verify
+            tight[r0 : r0 + 8, :] = loose[r1 : r1 + 8, :]
+        return jnp.concatenate([value[0:qrows], tight[qrows:crows, :]], axis=0)
+
     def statistics(peak, total):
         lane = lax.broadcasted_iota(jnp.int32, (srows, HEAD_DIM), 1)
         wide = jnp.where(lane == 0, peak, jnp.where(lane == 1, total, 0.0))
@@ -303,7 +304,7 @@
             )
         ]
 
-    def attend(b):
+    def attend(b, at):
         query = query_all[b].astype(F32)[0:qrows]
         row = lax.broadcasted_iota(jnp.int32, query.shape, 0)
         spread = jnp.concatenate(
@@ -338,7 +339,7 @@
             for kv in range(kv_local):
                 r0 = half * qrows + kv * grows
                 blocks.append(values[r0 : r0 + grows, kv * HEAD_DIM : (kv + 1) * HEAD_DIM])
-        send3[b] = jnp.concatenate(blocks, axis=0).astype(BF16)
+        send3[b] = compact(jnp.concatenate(blocks, axis=0), at).astype(BF16)
         sendml[b] = statistics(
             jnp.concatenate([t_peak, d_peak], axis=0),
             jnp.concatenate([t_total, d_total], axis=0),
@@ -357,8 +358,8 @@
 
             for copy in cache_copies(b):
                 copy.wait()
-        for b in several:
-            attend(b)
+        for at, b in enumerate(several):
+            attend(b, at)
         for b in several:
 
             @pl.when(jnp.logical_not(is_own(b)))
@@ -387,7 +388,7 @@
         moved = pltpu.roll(rows_all, rows_all.shape[0] - shift, 0)
         moved = jnp.where((vrow >= 0) & (vrow < shift), moved, 0.0).astype(BF16)
         values = jnp.dot(weights, moved, preferred_element_type=F32)
-        recv3[n_seq] = jnp.concatenate([values, values], axis=0).astype(BF16)
+        recv3[n_seq] = compact(jnp.concatenate([values, values], axis=0), 0).astype(BF16)
         recvml[n_seq] = statistics(
             jnp.concatenate([peak, peak], axis=0), jnp.concatenate([total, total], axis=0)
         )
@@ -410,49 +411,30 @@
         norm = jnp.sum(factor * l_all, axis=0, keepdims=True)
         norm = jnp.where(norm > 0.0, norm, 1.0)
         coefs[0:n_src, :] = factor / norm
-        coef_t[...] = coefs[...].T
-        acc = jnp.zeros((srows, HEAD_DIM), F32)
+        coef_t[0:crows, :] = compact(coefs[...].T[0:srows], 0)
+        acc = jnp.zeros((crows, HEAD_DIM), F32)
         for s in range(n_src):
-            acc = acc + coef_t[0:srows, s : s + 1] * recv3[s].astype(F32)
-        spare[0:srows, :] = acc
-        spare[srows : srows + 8, :] = jnp.zeros((8, HEAD_DIM), F32)
-        dense[...] = jnp.zeros_like(dense)
-        dense[0:qrows, :] = acc[0:qrows]
-        for h in range(heads):
-            r0, r1 = qrows + h * draft, qrows + h * verify
-            dense[r0 : r0 + 8, :] = spare[r1 : r1 + 8, :]
-        att[my_b] = dense[0:crows, :].astype(BF16)
-
-        copy_gather(att, s5_sem, r5_sem, my_b, partner).start()
-
-        @pl.loop(1, lines)
-        def _(off):
-            dst = 2 * lax.rem(line + off, lines) + side
-            copy_gather(att, s5_sem, r5_sem, my_b, dst).start()
+            acc = acc + coef_t[0:crows, s : s + 1] * recv3[s].astype(F32)
+        att[my_b] = acc.astype(BF16)
+        @pl.loop(0, lines)
+        def _(t):
+            far = jnp.where(2 * line < lines, lines - 1 - t, t)
+            for at in range(2):
+                dst = 2 * far + at
+
+                @pl.when(dst != me)
+                def _(dst=dst):
+                    copy_gather(att, s5_sem, r5_sem, my_b, dst).start()
 
     on_owner(owner_merge)
-
-    def copy_forward(b):
-        return pltpu.make_async_remote_copy(
-            src_ref=att.at[b],
-            dst_ref=att.at[b],
-            send_sem=f5_sem.at[b],
-            recv_sem=r5_sem.at[b],
-            device_id=(partner, hd),
-            device_id_type=MESH,
-        )
 
     @pl.loop(0, batch)
     def _(i):
-        b = gather_order(i)
+        b = use_order(i)
 
         @pl.when(jnp.logical_not(is_own(b)))
         def _():
-            copy_forward(b).wait_recv()
-
-        @pl.when(is_mine(b) & jnp.logical_not(is_own(b)))
-        def _():
-            copy_forward(b).start()
+            copy_gather(att, s5_sem, r5_sem, b, me).wait_recv()
 
         att32[pl.ds(pl.multiple_of(b * crows, 16), crows), :] = att[b].astype(F32)
 
@@ -488,15 +470,19 @@
         )
 
     wo_copy.wait()
-    for at in range(n_head):
-        r0, c0 = place(at)
+
+    @pl.loop(1, n_head + 1)
+    def _(off):
+        at = lax.rem(hd + off, n_head)
+        r0 = pl.multiple_of((at // col_parts) * part_rows, 16)
+        c0 = pl.multiple_of(lax.rem(at, col_parts) * part_cols, HEAD_DIM)
         send4[at] = jnp.dot(
-            x_buf[r0 : r0 + part_rows, :],
-            wo_buf[:, c0 : c0 + part_cols],
+            x_buf[pl.ds(r0, part_rows), :],
+            wo_buf[:, pl.ds(c0, part_cols)],
             preferred_element_type=F32,
         ).astype(BF16)
 
-        @pl.when(hd != at)
+        @pl.when(off < n_head)
         def _():
             copy4(at, hd).start()
 
@@ -556,19 +542,12 @@
             for copy in copies_up(b, me):
                 copy.wait_send()
 
-        @pl.when(is_mine(b) & jnp.logical_not(is_own(b)))
-        def _():
-            copy_forward(b).wait_send()
-
     def owner_sent():
         @pl.loop(1, n_seq)
         def _(off):
             dst = lax.rem(me + off, n_seq)
             copy_gather(query_all, s2_sem, r2_sem, my_b, dst).wait_send()
-
-            @pl.when((dst == partner) | (lax.rem(dst, 2) == side))
-            def _():
-                copy_gather(att, s5_sem, r5_sem, my_b, dst).wait_send()
+            copy_gather(att, s5_sem, r5_sem, my_b, dst).wait_send()
 
     on_owner(owner_sent)
 
@@ -645,8 +624,8 @@
             pltpu.VMEM((n_seq, rows1, HEAD_DIM), BF16),
             pltpu.VMEM((rows1, HEAD_DIM), BF16),
             pltpu.VMEM((batch, qpad, HEAD_DIM), BF16),
-            pltpu.VMEM((batch, srows, HEAD_DIM), BF16),
-            pltpu.VMEM((n_src, srows, HEAD_DIM), BF16),
+            pltpu.VMEM((batch, crows, HEAD_DIM), BF16),
+            pltpu.VMEM((n_src, crows, HEAD_DIM), BF16),
             pltpu.VMEM((batch, 2, lanes), F32),
             pltpu.VMEM((n_src, 2, lanes), F32),
             pltpu.VMEM((rows1, HEAD_DIM), F32),
@@ -656,8 +635,8 @@
             pltpu.VMEM((HEAD_DIM, lanes), F32),
             pltpu.VMEM((lanes, HEAD_DIM), F32),
             pltpu.VMEM((batch, crows, HEAD_DIM), BF16),
-            pltpu.VMEM((srows + 8, HEAD_DIM), F32),
-            pltpu.VMEM((crows + 8, HEAD_DIM), F32),
+            pltpu.VMEM((2, srows + 8, HEAD_DIM), F32),
+            pltpu.VMEM((2, crows + 8, HEAD_DIM), F32),
             pltpu.VMEM((batch * crows, HEAD_DIM), F32),
             pltpu.VMEM((all_rows, q_cols), BF16),
             pltpu.VMEM((n_head, part_rows, part_cols), BF16),
@@ -677,7 +656,6 @@
             dma((batch,)),
             dma((n_seq,)),
             dma((n_seq,)),
-            dma((batch,)),
             dma((batch,)),
             dma((n_head,)),
             dma((n_head,)),

time: 46.7 us -> 43.5 us (0.931)
  Pallas kernels: 44.7 us -> 41.4 us
    pallas_call x1, Pallas kernels: 44.7 us -> 41.4 us  [per_device(): pl.pallas_call(functools.partial(kernel, dims), out_shape=(pltpu.VMEM((ba...]
where the time goes in v6:
time: 43.5 us; the launch traced here: 43.3 us
  Pallas kernels  41.4 us (95%)
  local copies, waits for them, and re-layouts  1.27 us (3%)
  between operations  0.64 us (1%)
    pallas_call x1, Pallas kernels, per_device(): pl.pallas_call(functools.partial(kernel, dims), out_shape=(pltpu.VMEM((ba...  41.4 us
    unnamed x2, local copies, waits for them, and re-layouts  1.27 us

profile of v6, /device:TPU:0, one launch (start us, length us, event | category | flops | bytes accessed | tf_op | source)
XLA Modules:
  0.0 43.3 jit_solution(5530552387242853263)
XLA Ops:
  0.6 41.4 %verify_round.1 = (bf16[40,1024]{1,0:T(8,128)(2,1)S(1)}, bf16[8,4,1024]{2,1,0:T(4,128)(2,1)S(1)}) custom-call(bf16[40,1024]{1,0:T(8,128)(2,1)} %bitcast.7, f32[1,128]{1,0:T(1,128)} %constant.2.clone.inv_in, s32[8]{0:T(128)} %ctx_in.1, s32[8,8]{1,0:T(8,128)} %keep_in.1, bf16[1024,2048]{1,0:T(8,128)(2,1)} %wq.1, bf16[1024,256]{1,0:T(8,128)(2,1)} %wk.1, ...), custom_call_target="tpu_custom_call" | custom-call | tf_op jit(solution)/shard_map/verify_round/pallas_call | solution.py:604
  42.1 0.6 %copy.14 = bf16[8,5,1024]{2,0,1:T(8,128)(2,1)} copy(bf16[8,5,1024]{2,0,1:T(8,128)(2,1)S(1)} %bitcast.6) | data formatting | bytes 163840
  42.7 0.6 %copy.15 = bf16[8,4,1024]{2,1,0:T(4,128)(2,1)} copy(bf16[8,4,1024]{2,1,0:T(4,128)(2,1)S(1)} %get-tuple-element.7) | data formatting | bytes 131072

commit v7 on v6

--- a/solution.py
+++ b/solution.py
@@ -111,6 +111,10 @@
             return lax.rem(my_b + i, batch)
         return 2 * lax.rem(line + i // 2, lines) + lax.rem(side + i, 2)
 
+    def far_order(i):
+        t = i // 2
+        return 2 * jnp.where(2 * line < lines, lines - 1 - t, t) + lax.rem(i, 2)
+
     def is_own(b):
         return b * per == me
 
@@ -199,7 +203,7 @@
 
         @pl.loop(0, batch)
         def _(i):
-            b = lax.rem(my_b + 1 + i, batch)
+            b = far_order(i) if per == 1 else lax.rem(my_b + 1 + i, batch)
             rows = pl.ds(pl.multiple_of(b * rows1 + r0, 16), count)
             send1[b, r0 : r0 + count, :] = pack[rows, :].astype(BF16)
 
@@ -255,13 +259,13 @@
         qkv[...] = turned.astype(BF16)
         query_all[my_b] = turned[0 : query_all.shape[1]].astype(BF16)
 
-        @pl.loop(1, n_seq)
-        def _(off):
-            if per > 1:
-                dst = lax.rem(me + off, n_seq)
-            else:
-                dst = 2 * lax.rem(line + n_seq - off // 2, lines) + lax.rem(side + off, 2)
-            copy_gather(query_all, s2_sem, r2_sem, my_b, dst).start()
+        @pl.loop(0, n_seq)
+        def _(i):
+            dst = far_order(i)
+
+            @pl.when(dst != me)
+            def _():
+                copy_gather(query_all, s2_sem, r2_sem, my_b, dst).start()
 
     on_owner(owner_rotate)
 
@@ -416,15 +420,13 @@
         for s in range(n_src):
             acc = acc + coef_t[0:crows, s : s + 1] * recv3[s].astype(F32)
         att[my_b] = acc.astype(BF16)
-        @pl.loop(0, lines)
-        def _(t):
-            far = jnp.where(2 * line < lines, lines - 1 - t, t)
-            for at in range(2):
-                dst = 2 * far + at
-
-                @pl.when(dst != me)
-                def _(dst=dst):
-                    copy_gather(att, s5_sem, r5_sem, my_b, dst).start()
+        @pl.loop(0, n_seq)
+        def _(i):
+            dst = far_order(i)
+
+            @pl.when(dst != me)
+            def _():
+                copy_gather(att, s5_sem, r5_sem, my_b, dst).start()
 
     on_owner(owner_merge)
 

time: 43.5 us -> 44.5 us (1.023)
  Pallas kernels: 41.4 us -> 42.5 us
    pallas_call x1, Pallas kernels: 41.4 us -> 42.5 us  [per_device(): pl.pallas_call(functools.partial(kernel, dims), out_shape=(pltpu.VMEM((ba...]
where the time goes in v7:
time: 44.5 us; the launch traced here: 44.4 us
  Pallas kernels  42.5 us (96%)
  local copies, waits for them, and re-layouts  1.27 us (3%)
  between operations  0.64 us (1%)
    pallas_call x1, Pallas kernels, per_device(): pl.pallas_call(functools.partial(kernel, dims), out_shape=(pltpu.VMEM((ba...  42.5 us
    unnamed x2, local copies, waits for them, and re-layouts  1.27 us

profile of v7, /device:TPU:0, one launch (start us, length us, event | category | flops | bytes accessed | tf_op | source)
XLA Modules:
  0.0 44.4 jit_solution(5346000654933161910)
XLA Ops:
  0.6 42.5 %verify_round.1 = (bf16[40,1024]{1,0:T(8,128)(2,1)S(1)}, bf16[8,4,1024]{2,1,0:T(4,128)(2,1)S(1)}) custom-call(bf16[40,1024]{1,0:T(8,128)(2,1)} %bitcast.7, f32[1,128]{1,0:T(1,128)} %constant.2.clone.inv_in, s32[8]{0:T(128)} %ctx_in.1, s32[8,8]{1,0:T(8,128)} %keep_in.1, bf16[1024,2048]{1,0:T(8,128)(2,1)} %wq.1, bf16[1024,256]{1,0:T(8,128)(2,1)} %wk.1, ...), custom_call_target="tpu_custom_call" | custom-call | tf_op jit(solution)/shard_map/verify_round/pallas_call | solution.py:606
  43.1 0.6 %copy.14 = bf16[8,5,1024]{2,0,1:T(8,128)(2,1)} copy(bf16[8,5,1024]{2,0,1:T(8,128)(2,1)S(1)} %bitcast.6) | data formatting | bytes 163840
  43.7 0.6 %copy.15 = bf16[8,4,1024]{2,1,0:T(4,128)(2,1)} copy(bf16[8,4,1024]{2,1,0:T(4,128)(2,1)S(1)} %get-tuple-element.7) | data formatting | bytes 131072

commit v8 on v6

--- a/solution.py
+++ b/solution.py
@@ -207,10 +207,8 @@
             def _():
                 copy1(part, b, me).start()
 
-    early = rows1 // 2 // 16 * 16
-    parts = ((0, early), (early, rows1 - early))
-    sent_early = False
-    for at, (copy, (src, c0, width, d0)) in enumerate(zip(w_copies, pieces)):
+    parts = ((0, rows1),)
+    for copy, (src, c0, width, d0) in zip(w_copies, pieces):
         copy.wait()
         piece = jnp.dot(x_in, w_buf[:, d0 : d0 + width], preferred_element_type=F32)
         for s in range(width // HEAD_DIM):
@@ -219,11 +217,8 @@
                 pack[pl.ds(slot * verify + j, batch, stride=rows1), :] = piece[
                     j * batch : (j + 1) * batch, s * HEAD_DIM : (s + 1) * HEAD_DIM
                 ]
-        if not sent_early and (d0 + width) // HEAD_DIM * verify >= early:
-            sent_early = True
-            pl.semaphore_wait(barrier, n_seq - 1 + n_head - 1)
-            send_part(0)
-    send_part(1)
+    pl.semaphore_wait(barrier, n_seq - 1 + n_head - 1)
+    send_part(0)
 
     @pl.loop(0, batch)
     def _(i):
@@ -246,7 +241,7 @@
     def owner_rotate():
         def add(off, acc):
             src = lax.rem(me + off, n_seq)
-            for part in range(2):
+            for part in range(len(parts)):
                 copy1(part, my_b, src).wait_recv()
             return acc + recv1[src].astype(F32)
 
@@ -537,7 +532,7 @@
     def _(b):
         @pl.when(b * per != me)
         def _():
-            for part in range(2):
+            for part in range(len(parts)):
                 copy1(part, b, me).wait_send()
             for copy in copies_up(b, me):
                 copy.wait_send()
@@ -647,8 +642,8 @@
             dma,
             dma((batch,)),
             dma((batch,)),
-            dma((2, batch)),
-            dma((2, n_seq)),
+            dma((1, batch)),
+            dma((1, n_seq)),
             dma((n_seq,)),
             dma((batch,)),
             dma((batch,)),

time: 43.5 us -> 44.2 us (1.016)
  Pallas kernels: 41.4 us -> 42.2 us
    pallas_call x1, Pallas kernels: 41.4 us -> 42.2 us  [per_device(): pl.pallas_call(functools.partial(kernel, dims), out_shape=(pltpu.VMEM((ba...]
where the time goes in v8:
time: 44.2 us; the launch traced here: 44.1 us
  Pallas kernels  42.2 us (95%)
  local copies, waits for them, and re-layouts  1.27 us (3%)
  between operations  0.64 us (1%)
    pallas_call x1, Pallas kernels, per_device(): pl.pallas_call(functools.partial(kernel, dims), out_shape=(pltpu.VMEM((ba...  42.2 us
    unnamed x2, local copies, waits for them, and re-layouts  1.27 us

profile of v8, /device:TPU:0, one launch (start us, length us, event | category | flops | bytes accessed | tf_op | source)
XLA Modules:
  0.0 44.1 jit_solution(6783405367597025599)
XLA Ops:
  0.6 42.2 %verify_round.1 = (bf16[40,1024]{1,0:T(8,128)(2,1)S(1)}, bf16[8,4,1024]{2,1,0:T(4,128)(2,1)S(1)}) custom-call(bf16[40,1024]{1,0:T(8,128)(2,1)} %bitcast.7, f32[1,128]{1,0:T(1,128)} %constant.2.clone.inv_in, s32[8]{0:T(128)} %ctx_in.1, s32[8,8]{1,0:T(8,128)} %keep_in.1, bf16[1024,2048]{1,0:T(8,128)(2,1)} %wq.1, bf16[1024,256]{1,0:T(8,128)(2,1)} %wk.1, ...), custom_call_target="tpu_custom_call" | custom-call | tf_op jit(solution)/shard_map/verify_round/pallas_call | solution.py:599
  42.8 0.6 %copy.14 = bf16[8,5,1024]{2,0,1:T(8,128)(2,1)} copy(bf16[8,5,1024]{2,0,1:T(8,128)(2,1)S(1)} %bitcast.6) | data formatting | bytes 163840
  43.4 0.6 %copy.15 = bf16[8,4,1024]{2,1,0:T(4,128)(2,1)} copy(bf16[8,4,1024]{2,1,0:T(4,128)(2,1)S(1)} %get-tuple-element.7) | data formatting | bytes 131072
